TPU v7x, 32 devices: a whole 2x2x4 slice. The times are simulated.
32 devices in a mesh: dp: 8 (over y, x, core), fsdp: 4 (over z).
Axes of the slice: x: 2, y: 2, z: 4, core: 2. Of those that a mesh axis runs over, the one named last changes fastest.
Arguments:
- tokens: bfloat16 [32768, 768], P(('dp', 'fsdp'))
- cotangent: bfloat16 [32768, 768], P(('dp', 'fsdp')), may hold values from -6 to 6
- doc_lengths: int32 [32, 8], P(('dp', 'fsdp')), may hold values from 1 to 512, 1024 in all within a row
- block_slot: int32 [48], replicated, may hold values from 0 to 47, as said below
- matrices: float32 [48, 384, 384], P('dp', 'fsdp')
- vectors: float32 [9216], replicated
- vector_second: float32 [9216], replicated
- left_stat: float32 [48, 384, 384], P('dp', 'fsdp')
- right_stat: float32 [48, 384, 384], P('dp', 'fsdp')
- left_root: float32 [48, 384, 384], P('dp', 'fsdp')
- right_root: float32 [48, 384, 384], P('dp', 'fsdp')
Outputs:
- output: bfloat16 [32768, 768], P(('dp', 'fsdp'))
- x_grad: float32 [32768, 768], P(('dp', 'fsdp'))
- matrix_grad: float32 [48, 384, 384], P('dp', 'fsdp')
- left_new: float32 [48, 384, 384], P('dp', 'fsdp')
- right_new: float32 [48, 384, 384], P('dp', 'fsdp')
- matrix_new: float32 [48, 384, 384], P('dp', 'fsdp')
- vector_grad: float32 [9216], replicated
- second_new: float32 [9216], replicated
- vector_new: float32 [9216], replicated
- residual_scale: float32 [4], replicated
Inputs may be any that keep to these rules, and one draw needn't show every extreme that they name: block_slot is a permutation: block u of the layer's matrices, in the order of the steps, is stored in slot block_slot[u]. `doc_lengths`: each row's 8 document lengths sum to 1024.
All inputs are finite; a program needn't handle non-finite values.
Results may differ from a plain program's by a relative error of at most 0.0089.
Values may be sent and summed in bfloat16 or wider, within the bound.
No kernel may reach another device: no remote copies, remote signals or barrier semaphores. Data moves between devices by JAX's collectives and lax.ppermute only.
A program may use at most 320 MiB of HBM per device.

v0:
```python
import jax
import jax.numpy as jnp
from jax import lax
from jax.sharding import PartitionSpec as P

D = 768
HEADS = 12
HEAD_DIM = 64
FF = 3072


NORM_EPSILON = 1e-05
ROOT_EPSILON = 1e-08
DECAY = 0.5
MATRIX_RATE = 1.5
VECTOR_RATE = 0.1
MASKED = -1e30
HIGHEST = lax.Precision.HIGHEST


def layer_norm(values, gain, shift):
    center = values - jnp.mean(values, axis=-1, keepdims=True)
    spread = jnp.mean(center * center, axis=-1, keepdims=True)
    return center * lax.rsqrt(spread + NORM_EPSILON) * gain + shift


def norm_backward(values, gain, shift, grad):
    return jax.vjp(layer_norm, values, gain, shift)[1](grad)


def gelu_tanh(values):
    return jax.nn.gelu(values, approximate=True)


def split_vectors(packed):
    return [packed[index * D : (index + 1) * D] for index in range(8)] + [packed[8 * D :]]


def block_forward(inputs, blocks, grid_rows, grid_cols):
    count = inputs.shape[0]
    width = blocks.shape[-1]
    shaped = inputs.reshape(count, grid_rows, width)
    grid = blocks.reshape(grid_rows, grid_cols, width, width)
    return jnp.einsum("tik,ijkn->tjn", shaped, grid, preferred_element_type=jnp.float32).reshape(
        count, grid_cols * width
    )


def block_backward(grads, blocks, grid_rows, grid_cols):
    count = grads.shape[0]
    width = blocks.shape[-1]
    shaped = grads.reshape(count, grid_cols, width)
    grid = blocks.reshape(grid_rows, grid_cols, width, width)
    return jnp.einsum("tjn,ijkn->tik", shaped, grid, preferred_element_type=jnp.float32).reshape(
        count, grid_rows * width
    )


def block_weight_grad(inputs, grads, grid_rows, grid_cols):
    count = inputs.shape[0]
    width = inputs.shape[1] // grid_rows
    left = inputs.reshape(count, grid_rows, width)
    right = grads.reshape(count, grid_cols, width)
    return jnp.einsum("tik,tjn->ijkn", left, right, preferred_element_type=jnp.float32).reshape(
        grid_rows * grid_cols, width, width
    )


def allowed_block(lengths, first, span, seq_len):
    ends = jnp.cumsum(lengths)
    places = jnp.arange(seq_len, dtype=jnp.int32)
    doc_index = jnp.sum((places[:, None] >= ends[None, :]).astype(jnp.int32), axis=1)
    query_doc = doc_index[first : first + span]
    query_place = places[first : first + span]
    return (query_doc[:, None] == doc_index[None, :]) & (places[None, :] <= query_place[:, None])


def head_view(rows_in):
    return rows_in.reshape(rows_in.shape[0], HEADS, HEAD_DIM)


def block_scores(query_heads, key_heads, allowed):
    raw = jnp.einsum("qhd,khd->hqk", query_heads, key_heads, preferred_element_type=jnp.float32)
    return jnp.where(allowed[None], raw * HEAD_DIM ** (-0.5), MASKED)


def attend_forward(operands):
    queries, key_rows, value_rows, lengths = operands
    seq_len = queries.shape[0]
    span = min(512, seq_len)
    query_heads = head_view(queries)
    key_heads = head_view(key_rows)
    value_heads = head_view(value_rows)
    mixed_parts = []
    total_parts = []
    for first in range(0, seq_len, span):
        scores = block_scores(
            query_heads[first : first + span],
            key_heads,
            allowed_block(lengths, first, span, seq_len),
        )
        peak = jnp.max(scores, axis=-1, keepdims=True)
        weights = jnp.exp(scores - peak)
        total = jnp.sum(weights, axis=-1, keepdims=True)
        probs = (weights / total).astype(jnp.bfloat16)
        mixed_parts.append(
            jnp.einsum("hqk,khd->qhd", probs, value_heads, preferred_element_type=jnp.float32)
        )
        total_parts.append((peak + jnp.log(total))[:, :, 0])
    mixed = jnp.concatenate(mixed_parts, axis=0)
    return (mixed.reshape(seq_len, HEADS * HEAD_DIM), jnp.concatenate(total_parts, axis=1))


def attend_backward(operands):
    queries, key_rows, value_rows, lengths, log_totals, grad_mixed = operands
    seq_len = queries.shape[0]
    span = min(512, seq_len)
    scale = HEAD_DIM ** (-0.5)
    query_heads = head_view(queries)
    key_heads = head_view(key_rows)
    value_heads = head_view(value_rows)
    grad_heads = head_view(grad_mixed)
    query_grads = []
    key_grad = jnp.zeros(key_heads.shape, jnp.float32)
    value_grad = jnp.zeros(value_heads.shape, jnp.float32)
    for first in range(0, seq_len, span):
        query_block = query_heads[first : first + span]
        grad_block = grad_heads[first : first + span]
        scores = block_scores(query_block, key_heads, allowed_block(lengths, first, span, seq_len))
        probs = jnp.exp(scores - log_totals[:, first : first + span, None])
        grad_probs = jnp.einsum(
            "qhd,khd->hqk", grad_block, value_heads, preferred_element_type=jnp.float32
        )
        inner = jnp.sum(probs * grad_probs, axis=-1, keepdims=True)
        grad_scores = (probs * (grad_probs - inner)).astype(jnp.bfloat16)
        query_grads.append(
            jnp.einsum("hqk,khd->qhd", grad_scores, key_heads, preferred_element_type=jnp.float32)
            * scale
        )
        key_grad = (
            key_grad
            + jnp.einsum(
                "hqk,qhd->khd", grad_scores, query_block, preferred_element_type=jnp.float32
            )
            * scale
        )
        value_grad = value_grad + jnp.einsum(
            "hqk,qhd->khd",
            probs.astype(jnp.bfloat16),
            grad_block,
            preferred_element_type=jnp.float32,
        )
    width = HEADS * HEAD_DIM
    query_grad = jnp.concatenate(query_grads, axis=0).reshape(seq_len, width)
    return (query_grad, key_grad.reshape(seq_len, width), value_grad.reshape(seq_len, width))


def per_device(
    tokens,
    cotangent,
    doc_lengths,
    block_slot,
    matrices,
    vectors,
    vector_second,
    left_stat,
    right_stat,
    left_root,
    right_root,
):
    dp_count = lax.axis_size("dp")
    fsdp_count = lax.axis_size("fsdp")
    own_blocks, own_rows, width = matrices.shape
    row_grid = D // width
    ff_grid = FF // width
    bounds = [
        0,
        3 * row_grid * row_grid,
        4 * row_grid * row_grid,
        4 * row_grid * row_grid + row_grid * ff_grid,
        own_blocks * dp_count,
    ]
    slot_place = block_slot % own_blocks * dp_count + block_slot // own_blocks
    low_shards = matrices.astype(jnp.bfloat16)
    gathered = lax.all_gather(low_shards, ("dp", "fsdp"), axis=1, tiled=True)
    used = jnp.take(gathered.reshape(own_blocks * dp_count, width, width), slot_place, axis=0)
    w_qkv, w_out, w_fc, w_proj = [used[bounds[index] : bounds[index + 1]] for index in range(4)]
    ln1_gain, ln1_shift, q_bias, v_bias, out_bias, ln2_gain, ln2_shift, proj_bias, fc_bias = (
        split_vectors(vectors)
    )
    count = tokens.shape[0]
    rows_here = doc_lengths.shape[0]
    seq_len = count // rows_here
    inputs = tokens.astype(jnp.float32)
    normed1 = layer_norm(inputs, ln1_gain, ln1_shift).astype(jnp.bfloat16)
    bias_qkv = jnp.concatenate([q_bias, jnp.zeros_like(q_bias), v_bias])
    projected = (block_forward(normed1, w_qkv, row_grid, 3 * row_grid) + bias_qkv).astype(
        jnp.bfloat16
    )
    parts = projected.reshape(rows_here, seq_len, 3 * D)
    heads_in = (parts[:, :, :D], parts[:, :, D : 2 * D], parts[:, :, 2 * D :], doc_lengths)
    mixed, log_totals = lax.map(attend_forward, heads_in)
    attended = mixed.reshape(count, D).astype(jnp.bfloat16)
    attn_out = block_forward(attended, w_out, row_grid, row_grid) + out_bias
    middle = inputs + attn_out
    normed2 = layer_norm(middle, ln2_gain, ln2_shift).astype(jnp.bfloat16)
    pre_act = block_forward(normed2, w_fc, row_grid, ff_grid) + fc_bias
    hidden = gelu_tanh(pre_act).astype(jnp.bfloat16)
    mlp_out = block_forward(hidden, w_proj, ff_grid, row_grid) + proj_bias
    result = middle + mlp_out
    regathered = lax.all_gather(low_shards, ("dp", "fsdp"), axis=1, tiled=True)
    used_back = jnp.take(
        regathered.reshape(own_blocks * dp_count, width, width), slot_place, axis=0
    )
    back_qkv, back_out, back_fc, back_proj = [
        used_back[bounds[index] : bounds[index + 1]] for index in range(4)
    ]
    grad_result = cotangent.astype(jnp.float32)
    proj_grad = block_weight_grad(hidden, cotangent, ff_grid, row_grid)
    proj_bias_grad = jnp.sum(grad_result, axis=0)
    grad_hidden = block_backward(cotangent, back_proj, ff_grid, row_grid)
    grad_pre = jax.vjp(gelu_tanh, pre_act)[1](grad_hidden)[0].astype(jnp.bfloat16)
    fc_grad = block_weight_grad(normed2, grad_pre, row_grid, ff_grid)
    fc_bias_grad = jnp.sum(grad_pre.astype(jnp.float32), axis=0)
    grad_normed2 = block_backward(grad_pre, back_fc, row_grid, ff_grid)
    grad_from2, ln2_gain_grad, ln2_shift_grad = norm_backward(
        middle, ln2_gain, ln2_shift, grad_normed2
    )
    grad_middle = grad_result + grad_from2
    grad_branch = grad_middle.astype(jnp.bfloat16)
    out_grad = block_weight_grad(attended, grad_branch, row_grid, row_grid)
    out_bias_grad = jnp.sum(grad_branch.astype(jnp.float32), axis=0)
    grad_attended = block_backward(grad_branch, back_out, row_grid, row_grid).astype(jnp.bfloat16)
    heads_back = heads_in + (log_totals, grad_attended.reshape(rows_here, seq_len, D))
    query_grad, key_grad, value_grad = lax.map(attend_backward, heads_back)
    grad_projected = (
        jnp.concatenate([query_grad, key_grad, value_grad], axis=-1)
        .reshape(count, 3 * D)
        .astype(jnp.bfloat16)
    )
    qkv_grad = block_weight_grad(normed1, grad_projected, row_grid, 3 * row_grid)
    projected_sums = jnp.sum(grad_projected.astype(jnp.float32), axis=0)
    grad_normed1 = block_backward(grad_projected, back_qkv, row_grid, 3 * row_grid)
    grad_from1, ln1_gain_grad, ln1_shift_grad = norm_backward(
        inputs, ln1_gain, ln1_shift, grad_normed1
    )
    x_grad = grad_middle + grad_from1
    vector_local = jnp.concatenate(
        [
            ln1_gain_grad,
            ln1_shift_grad,
            projected_sums[:D],
            projected_sums[2 * D :],
            out_bias_grad,
            ln2_gain_grad,
            ln2_shift_grad,
            proj_bias_grad,
            fc_bias_grad,
        ]
    )
    grads_used = jnp.concatenate([qkv_grad, out_grad, fc_grad, proj_grad], axis=0)
    grads_laid = jnp.take(grads_used, jnp.argsort(slot_place), axis=0).reshape(
        own_blocks, dp_count * width, width
    )
    fsdp_index = lax.axis_index("fsdp")
    grad_rows = lax.psum_scatter(grads_laid, ("dp", "fsdp"), scatter_dimension=1, tiled=True)
    grad_whole = lax.all_gather(grad_rows, "fsdp", axis=1, tiled=True)
    grad_cols = lax.dynamic_slice_in_dim(grad_whole, fsdp_index * own_rows, own_rows, 2)
    left_new = DECAY * left_stat + (1.0 - DECAY) * jnp.einsum(
        "brk,bjk->brj", grad_rows, grad_whole, precision=HIGHEST
    )
    right_new = DECAY * right_stat + (1.0 - DECAY) * jnp.einsum(
        "bkr,bkj->brj", grad_cols, grad_whole, precision=HIGHEST
    )
    right_whole = lax.all_gather(right_root, "fsdp", axis=1, tiled=True)
    half = jnp.einsum("brk,bkj->brj", left_root, grad_whole, precision=HIGHEST)
    update = jnp.einsum("brk,bkj->brj", half, right_whole, precision=HIGHEST)
    matrix_new = matrices - MATRIX_RATE * update
    square_terms = jnp.stack(
        [
            jnp.sum(middle * middle),
            jnp.sum(result * result),
            jnp.sum(attn_out * attn_out),
            jnp.sum(mlp_out * mlp_out),
        ]
    )
    vector_grad, square_sums = lax.psum((vector_local, square_terms), ("dp", "fsdp"))
    residual_scale = jnp.sqrt(square_sums / (count * dp_count * fsdp_count * D))
    second_new = DECAY * vector_second + (1.0 - DECAY) * vector_grad * vector_grad
    vector_new = vectors - VECTOR_RATE * vector_grad / (jnp.sqrt(second_new) + ROOT_EPSILON)
    return (
        result.astype(jnp.bfloat16),
        x_grad,
        grad_rows,
        left_new,
        right_new,
        matrix_new,
        vector_grad,
        second_new,
        vector_new,
        residual_scale,
    )


def solution(mesh):
    return jax.shard_map(
        per_device,
        mesh=mesh,
        in_specs=(
            P(("dp", "fsdp"), None),
            P(("dp", "fsdp"), None),
            P(("dp", "fsdp"), None),
            P(),
            P("dp", "fsdp", None),
            P(),
            P(),
            P("dp", "fsdp", None),
            P("dp", "fsdp", None),
            P("dp", "fsdp", None),
            P("dp", "fsdp", None),
        ),
        out_specs=(
            P(("dp", "fsdp"), None),
            P(("dp", "fsdp"), None),
            P("dp", "fsdp", None),
            P("dp", "fsdp", None),
            P("dp", "fsdp", None),
            P("dp", "fsdp", None),
            P(),
            P(),
            P(),
            P(),
        ),
        check_vma=False,
    )
```

profile of v0, /device:TPU:0, one launch (start us, length us, event | category | flops | bytes accessed | tf_op | source)
XLA Modules:
  0.0 1051.1 jit_solution(4402911524078104658)
XLA Ops:
  23.0 94.6 %all-gather.4.cloned.1.call-done = bf16[6,3072,384]{2,1,0:T(8,128)(2,1)} async-done(((bf16[6,96,384]{2,1,0:T(8,128)(2,1)}), bf16[6,3072,384]{2,1,0:T(8,128)(2,1)}) %all-gather.4.cloned.1.call-update) | async-done | bytes 14155792 | tf_op jit(solution)/shard_map/all_gather | solution.py:185
  117.7 12.4 %gather_fusion.1 = bf16[48,384,384]{2,1,0:T(8,128)(2,1)} fusion(bf16[48,384,384]{2,1,0:T(8,128)(2,1)} %bitcast.240, s32[1024]{0:T(1024)S(1)} %pad_clamp_fusion.1), kind=kCustom, calls=%fused_computation.clone | custom fusion | bytes 28311744 | tf_op jit(solution)/shard_map/jit(_take)/gather | solution.py:186
  130.1 7.8 broadcast_select_fusion
  137.8 5.0 copy-done.6
  145.0 6.1 copy.101
  151.1 6.1 fusion.32
  162.8 8.9 fusion.90
  178.9 12.4 %fusion.20 = (f32[12,512]{1,0:T(8,128)S(1)}, f32[12,512,1024]{2,1,0:T(8,128)}) fusion(pred[512,1024]{1,0:T(8,128)(4,1)S(1)} %get-tuple-element.141, bf16[512,12,64]{0,2,1:T(8,128)(2,1)} %bitcast.248, bf16[1024,12,64]{0,2,1:T(8,128)(2,1)S(1)} %bitcast.227), kind=kOutput, calls=%fused_computation.43 | convolution fusion | flops 824174592 | bytes 28073984 | tf_op jit(solution)/shard_map/while/body/eval_jaxpr/qhd,khd->hqk/dot_general | solution.py:83
  191.3 12.3 %fusion = f32[12,512]{1,0:T(8,128)S(1)} fusion(f32[12,512]{1,0:T(8,128)S(1)} %get-tuple-element.147, f32[12,512,1024]{2,1,0:T(8,128)} %get-tuple-element.148, pred[512,1024]{1,0:T(8,128)(4,1)S(1)} %get-tuple-element.141), kind=kLoop, calls=%fused_computation.16 | loop fusion | flops 25159680 | bytes 25739264 | tf_op jit(solution)/shard_map/while/body/eval_jaxpr/reduce_sum | solution.py:104
  206.7 8.5 fusion.58
  217.5 12.0 %fusion.21 = (f32[12,512]{1,0:T(8,128)S(1)}, f32[12,512,1024]{2,1,0:T(8,128)}) fusion(pred[512,1024]{1,0:T(8,128)(4,1)S(1)} %get-tuple-element.142, bf16[512,12,64]{0,2,1:T(8,128)(2,1)} %bitcast.244, bf16[1024,12,64]{0,2,1:T(8,128)(2,1)S(1)} %bitcast.228), kind=kOutput, calls=%fused_computation.44 | convolution fusion | flops 824174592 | bytes 28073984 | tf_op jit(solution)/shard_map/while/body/eval_jaxpr/qhd,khd->hqk/dot_general | solution.py:83
  229.5 12.3 %fusion.1 = f32[12,512]{1,0:T(8,128)S(1)} fusion(f32[12,512]{1,0:T(8,128)S(1)} %get-tuple-element.145, f32[12,512,1024]{2,1,0:T(8,128)} %get-tuple-element.146, pred[512,1024]{1,0:T(8,128)(4,1)S(1)} %get-tuple-element.142), kind=kLoop, calls=%fused_computation.17 | loop fusion | flops 25159680 | bytes 25739264 | tf_op jit(solution)/shard_map/while/body/eval_jaxpr/reduce_sum | solution.py:104
  244.9 8.5 fusion.57
  258.6 14.7 %copy.109 = bf16[4,384,384]{1,2,0:T(8,128)(2,1)} copy(bf16[4,384,384]{2,1,0:T(8,128)(2,1)} %slice.156) | data formatting | bytes 2359296 | tf_op jit(solution)/shard_map/slice | solution.py:187
  279.6 10.4 fusion.55
  290.0 12.6 %copy.151 = f32[1024,3072]{1,0:T(8,128)} copy(f32[1024,3072]{0,1:T(8,128)} %bitcast.241) | data formatting | bytes 25165824 | tf_op jit(solution)/shard_map/reshape | solution.py:54
  302.6 6.6 copy.110
  309.2 5.1 copy.118
  314.3 6.6 copy.112
  324.7 19.8 %convert_reduce_fusion = (f32[3072]{0:T(1024)}, bf16[1024,3072]{1,0:T(8,128)(2,1)}, bf16[1024,3072]{1,0:T(8,128)(2,1)S(1)}) fusion(f32[1024,3072]{1,0:T(8,128)} %copy.151, f32[3072]{0:T(1024)S(1)} %slice-done.2, bf16[1024,2,384]{0,2,1:T(8,128)(2,1)} %bitcast.275, bf16[3072,2,384]{2,0,1:T(8,128)(2,1)} %bitcast.263), kind=kOutput, calls=%fused_computation.33 | convolution fusion | flops 4910478336 | bytes 31481856 | tf_op jit(solution)/shard_map/tik,ijkn->tjn/dot_general | solution.py:44
  344.5 10.9 %fusion.22 = f32[1024,768,1]{0,1,2:T(8,128)S(1)} fusion(bf16[768,8,384]{2,0,1:T(8,128)(2,1)} %bitcast.262, bf16[128,8,8,384]{3,2,1,0:T(8,128)(2,1)} %bitcast.252), kind=kOutput, calls=%fused_computation.45 | convolution fusion | flops 4831838208 | bytes 14155776 | tf_op jit(solution)/shard_map/tjn,ijkn->tik/dot_general | solution.py:54
  355.5 9.2 multiply_reduce_fusion.4
  371.0 18.3 %multiply_reduce_fusion.1 = (f32[12,512]{1,0:T(8,128)}, f32[12,512,1024]{2,1,0:T(8,128)}) fusion(f32[12,512]{1,0:T(8,128)S(1)} %copy-done.46, f32[12,512,1024]{2,1,0:T(8,128)} %get-tuple-element.148, pred[512,1024]{1,0:T(8,128)(4,1)S(1)} %copy-done.22, bf16[512,12,64]{0,2,1:T(8,128)(2,1)} %bitcast.266, bf16[1024,12,64]{0,2,1:T(8,128)(2,1)S(1)} %bitcast.238), kind=kOutput, calls=%fused_computation.8 | convolution fusion | flops 836757504 | bytes 53264384 | tf_op jit(solution)/shard_map/while/body/eval_jaxpr/qhd,khd->hqk/dot_general | solution.py:131
  389.3 18.4 %multiply_reduce_fusion = (f32[12,512]{1,0:T(8,128)}, f32[12,512,1024]{2,1,0:T(8,128)}) fusion(f32[12,512]{1,0:T(8,128)} %log_add_fusion, f32[12,512,1024]{2,1,0:T(8,128)} %get-tuple-element.146, pred[512,1024]{1,0:T(8,128)(4,1)S(1)} %get-tuple-element.142, bf16[512,12,64]{0,2,1:T(8,128)(2,1)} %bitcast.268, bf16[1024,12,64]{0,2,1:T(8,128)(2,1)S(1)} %bitcast.239), kind=kOutput, calls=%fused_computation.5 | convolution fusion | flops 836757504 | bytes 53264384 | tf_op jit(solution)/shard_map/while/body/eval_jaxpr/qhd,khd->hqk/dot_general | solution.py:131
  407.7 42.5 %multiply_convert_fusion = (bf16[12,512,1024]{2,1,0:T(8,128)(2,1)}, bf16[12,512,1024]{2,1,0:T(8,128)(2,1)}) fusion(f32[12,512,1024]{2,1,0:T(8,128)} %get-tuple-element.152, f32[12,512]{1,0:T(8,128)} %get-tuple-element.151, f32[12,512]{1,0:T(8,128)} %log_add_fusion, f32[12,512,1024]{2,1,0:T(8,128)} %get-tuple-element.146, ...), kind=kLoop, calls=%fused_computation.4 | loop fusion | flops 75497472 | bytes 126976000 | tf_op jit(solution)/shard_map/while/body/eval_jaxpr/convert_element_type | solution.py:135
  450.3 9.6 multiply_bitcast_fusion.1
  459.8 7.0 fusion.97
  466.9 11.6 %fusion.11 = f32[12,64,1024]{2,1,0:T(8,128)S(1)} fusion(bf16[512,12,64]{0,2,1:T(8,128)(2,1)S(1)} %bitcast.269, f32[12,512]{1,0:T(8,128)S(1)} %copy-done.47, f32[12,512,1024]{2,1,0:T(8,128)} %get-tuple-element.146, pred[512,1024]{1,0:T(8,128)(4,1)S(1)} %get-tuple-element.142), kind=kOutput, calls=%fused_computation.30 | convolution fusion | flops 830472192 | bytes 29646848 | tf_op jit(solution)/shard_map/while/body/eval_jaxpr/hqk,qhd->khd/dot_general | solution.py:147
  478.5 9.6 multiply_bitcast_fusion
  488.1 6.9 add_multiply_fusion
  495.1 13.0 %fusion.52 = bf16[12,64,1024]{2,1,0:T(8,128)(2,1)} fusion(f32[12,64,1024]{2,1,0:T(8,128)S(1)} %fusion.11, bf16[512,12,64]{0,2,1:T(8,128)(2,1)S(1)} %bitcast.267, f32[12,512]{1,0:T(8,128)S(1)} %copy-done.46, f32[12,512,1024]{2,1,0:T(8,128)} %get-tuple-element.148, pred[512,1024]{1,0:T(8,128)(4,1)S(1)} %copy-done.22), kind=kOutput, calls=%fused_computation.101 | convolution fusion | flops 832045056 | bytes 31219712 | tf_op jit(solution)/shard_map/while/body/eval_jaxpr/hqk,qhd->khd/dot_general | solution.py:147
  513.9 4.5 copy.165
  518.5 8.3 fusion.39
  526.8 9.8 copy.130
  541.3 7.2 convolution_bitcast_fusion
  548.6 8.1 copy.126
  556.6 4.5 copy.166
  561.2 7.8 fusion.28
  569.0 18.4 %pad_maximum_fusion = f32[48,384,384]{2,1,0:T(8,128)} fusion(f32[16,384,384]{2,1,0:T(8,128)} %bitcast.247, f32[16,384,384]{2,1,0:T(8,128)} %bitcast.231, f32[4,384,384]{2,1,0:T(8,128)S(1)} %bitcast.246, f32[12,384,384]{2,1,0:T(8,128)} %bitcast.233), kind=kLoop, calls=%fused_computation.2 | loop fusion | flops 21233664 | bytes 56623104 | tf_op jit(solution)/shard_map/concatenate | solution.py:261
  587.4 21.1 %gather_fusion = f32[48,384,384]{2,1,0:T(8,128)} fusion(f32[48,384,384]{2,1,0:T(8,128)} %pad_maximum_fusion, s32[1024]{0:T(1024)} %pad_clamp_fusion), kind=kCustom, calls=%fused_computation.1 | custom fusion | bytes 56623296 | tf_op jit(solution)/shard_map/jit(_take)/gather | solution.py:262
  608.5 21.7 %bitcast_select_fusion = f32[6,3072,384]{2,1,0:T(8,128)} fusion(pred[6,3072]{1,0:T(8,128)(4,1)S(1)} %bitcast.283, f32[6,3072,384]{2,1,0:T(8,128)} %bitcast.225), kind=kLoop, calls=%fused_computation.3 | loop fusion | flops 7077888 | bytes 56641536 | tf_op jit(solution)/shard_map/jit(_take)/select_n | solution.py:262
  630.2 261.8 %reduce-scatter.2.cloned.1.call-done = f32[6,96,384]{2,1,0:T(8,128)} async-done(((f32[6,3072,384]{2,1,0:T(8,128)}), f32[6,96,384]{2,1,0:T(8,128)}) %reduce-scatter.2.cloned.1.call-update) | async-done | bytes 884752 | tf_op jit(solution)/shard_map/reduce_scatter | solution.py:266
  895.0 7.9 fusion.96
  923.2 43.2 %all-reduce = (f32[9216]{0:T(1024)S(1)}, f32[4]{0:T(128)S(1)}) all-reduce(f32[9216]{0:T(1024)S(1)} %constant_dynamic-update-slice_fusion, f32[4]{0:T(128)S(1)} %pad_maximum_fusion.6), channel_id=1, replica_groups=mesh['dp'=8,'fsdp'=4] {'dp','fsdp'}, use_global_device_ids=true, to_apply=%region_26.28 | all-reduce | flops 9220 | bytes 73760 | tf_op jit(solution)/shard_map/psum | solution.py:287
  967.7 4.7 fusion.98
  972.4 5.9 fusion.63
  978.4 56.4 %all-gather.8.cloned.1.call-done = f32[6,384,384]{2,1,0:T(8,128)} async-done(((f32[6,96,384]{2,1,0:T(8,128)}), f32[6,384,384]{2,1,0:T(8,128)}) %all-gather.8.cloned.1.call-update) | async-done | bytes 3538960 | tf_op jit(solution)/shard_map/all_gather | solution.py:275
  1034.8 5.5 fusion.62
  (242 shorter events, 99.3 us)
Async XLA Ops:
  7.2 960.5 %copy-start = (f32[6,96,384]{2,1,0:T(8,128)S(1)}, f32[6,96,384]{2,1,0:T(8,128)}, u32[]{:S(2)}) copy-start(f32[6,96,384]{2,1,0:T(8,128)} %param.22) | copy-start | bytes 2654212
  7.2 110.5 %all-gather.4.cloned.1.call-start = ((), (), s32[]{:S(2)}) async-start(), calls=%async_computation.1 | async-start | bytes 14598144 | tf_op jit(solution)/shard_map/all_gather | solution.py:185
  9.3 7.9 copy-start.72
  9.3 8.7 copy-start.48
  9.3 882.8 %reduce-scatter.2.cloned.1.call-start = ((), (), s32[]{:S(2)}) async-start(), calls=%async_computation.2 | async-start | bytes 29196288 | tf_op jit(solution)/shard_map/reduce_scatter | solution.py:266
  11.1 10.7 %copy-start.3 = (bf16[1024,768]{0,1:T(8,128)(2,1)}, bf16[1024,768]{0,1:T(8,128)(2,1)S(1)}, u32[]{:S(2)}) copy-start(bf16[1024,768]{0,1:T(8,128)(2,1)S(1)} %copy.100) | copy-start | bytes 4718596
  23.0 181.2 %copy-start.21 = (pred[512,1024]{1,0:T(8,128)(4,1)}, pred[512,1024]{1,0:T(8,128)(4,1)S(1)}, u32[]{:S(2)}) copy-start(pred[512,1024]{1,0:T(8,128)(4,1)S(1)} %get-tuple-element.141) | copy-start | bytes 1572868
  137.8 5.1 copy-start.6
  145.0 6.1 copy-start.37
  173.5 44.0 %copy-start.8 = (bf16[1,1024,768]{1,2,0:T(8,128)(2,1)}, bf16[1,1024,768]{1,2,0:T(8,128)(2,1)S(1)}, u32[]{:S(2)}) copy-start(bf16[1,1024,768]{1,2,0:T(8,128)(2,1)S(1)} %copy.105) | copy-start | bytes 4718596
  178.9 25.3 %copy-start.16 = (bf16[1,1024,768]{1,2,0:T(8,128)(2,1)S(1)}, bf16[1,1024,768]{1,2,0:T(8,128)(2,1)}, u32[]{:S(2)}) copy-start(bf16[1,1024,768]{1,2,0:T(8,128)(2,1)} %copy.103) | copy-start | bytes 4718596
  191.3 15.4 %copy-start.1 = (f32[12,512,1024]{2,1,0:T(8,128)S(1)}, f32[12,512,1024]{2,1,0:T(8,128)}, u32[]{:S(2)}) copy-start(f32[12,512,1024]{2,1,0:T(8,128)} %get-tuple-element.148) | copy-start | bytes 75497472
  217.5 24.3 %copy-start.17 = (bf16[1,1024,768]{1,2,0:T(8,128)(2,1)S(1)}, bf16[1,1024,768]{1,2,0:T(8,128)(2,1)}, u32[]{:S(2)}) copy-start(bf16[1,1024,768]{1,2,0:T(8,128)(2,1)} %copy.103) | copy-start | bytes 4718596
  229.5 15.4 %copy-start.2 = (f32[12,512,1024]{2,1,0:T(8,128)S(1)}, f32[12,512,1024]{2,1,0:T(8,128)}, u32[]{:S(2)}) copy-start(f32[12,512,1024]{2,1,0:T(8,128)} %get-tuple-element.146) | copy-start | bytes 75497472
  253.4 19.9 %copy-start.4 = (bf16[1024,768]{0,1:T(8,128)(2,1)S(1)}, bf16[1024,768]{0,1:T(8,128)(2,1)}, u32[]{:S(2)}) copy-start(bf16[1024,768]{0,1:T(8,128)(2,1)} %copy-done.3) | copy-start | bytes 4718596
  253.4 19.9 %copy-start.68 = (f32[768]{0:T(1024)S(1)}, f32[768]{0:T(1024)}, u32[]{:S(2)}) copy-start(f32[768]{0:T(1024)} %get-tuple-element.135) | copy-start | bytes 9220
  273.3 6.2 copy-start.35
  314.3 6.6 copy-start.59
  314.3 6.6 copy-start.64
  321.0 34.5 %slice-start = ((s8[4718592]{0:T(1024)(128)(4,1)}), s8[4194304]{0:T(1024)(128)(4,1)S(1)}, s32[]{:S(2)}) async-start(s8[4718592]{0:T(1024)(128)(4,1)} %bitcast.259), calls=%async_computation.5 | async-start | bytes 8388608
  324.7 30.8 %slice-start.1 = ((s8[4718592]{0:T(1024)(128)(4,1)}), s8[524288]{0:T(1024)(128)(4,1)S(1)}, s32[]{:S(2)}) async-start(s8[4718592]{0:T(1024)(128)(4,1)} %bitcast.259), calls=%async_computation.6 | async-start | bytes 1048576
  344.5 10.9 %copy-start.27 = (bf16[1024,3072]{1,0:T(8,128)(2,1)}, bf16[1024,3072]{1,0:T(8,128)(2,1)S(1)}, u32[]{:S(2)}) copy-start(bf16[1024,3072]{1,0:T(8,128)(2,1)S(1)} %get-tuple-element.122) | copy-start | bytes 18874372
  344.5 10.9 %copy-start.13 = (f32[1024,768]{0,1:T(8,128)S(1)}, f32[1024,768]{0,1:T(8,128)}, u32[]{:S(2)}) copy-start(f32[1024,768]{0,1:T(8,128)} %copy-done.12) | copy-start | bytes 9437188
  344.5 10.9 %copy-start.67 = (f32[768]{0:T(1024)S(1)}, f32[768]{0:T(1024)}, u32[]{:S(2)}) copy-start(f32[768]{0:T(1024)} %get-tuple-element.140) | copy-start | bytes 9220
  407.7 42.5 %copy-start.9 = (bf16[1,1024,768]{1,2,0:T(8,128)(2,1)S(1)}, bf16[1,1024,768]{1,2,0:T(8,128)(2,1)}, u32[]{:S(2)}) copy-start(bf16[1,1024,768]{1,2,0:T(8,128)(2,1)} %copy-done.8) | copy-start | bytes 4718596
  450.2 9.6 copy-start.26
  459.8 7.0 copy-start.33
  459.8 7.0 copy-start.47
  478.5 9.6 copy-start.24
  488.1 7.0 copy-start.32
  495.0 13.0 %copy-start.42 = (bf16[1024,768]{0,1:T(8,128)(2,1)S(1)}, bf16[1024,768]{0,1:T(8,128)(2,1)}, u32[]{:S(2)}) copy-start(bf16[1024,768]{0,1:T(8,128)(2,1)} %copy-done.41) | copy-start | bytes 4718596
  495.0 13.0 %copy-start.44 = (bf16[512,2,384]{2,0,1:T(8,128)(2,1)S(1)}, bf16[512,2,384]{2,0,1:T(8,128)(2,1)}, u32[]{:S(2)}) copy-start(bf16[512,2,384]{2,0,1:T(8,128)(2,1)} %copy.107) | copy-start | bytes 2359300
  495.1 13.0 %copy-start.45 = (bf16[512,2,384]{2,0,1:T(8,128)(2,1)S(1)}, bf16[512,2,384]{2,0,1:T(8,128)(2,1)}, u32[]{:S(2)}) copy-start(bf16[512,2,384]{2,0,1:T(8,128)(2,1)} %copy.108) | copy-start | bytes 2359300
  526.8 9.8 copy-start.31
  561.2 7.8 copy-start.25
  587.4 21.1 %copy-start.54 = (pred[1,6,8,384]{3,1,2,0:T(8,128)(4,1)S(1)}, pred[1,6,8,384]{3,1,2,0:T(8,128)(4,1)}, u32[]{:S(2)}) copy-start(pred[1,6,8,384]{3,1,2,0:T(8,128)(4,1)} %copy.164) | copy-start | bytes 55300
  630.2 337.5 %all-gather.6.cloned.1.call-start = ((), (), s32[]{:S(2)}) async-start(), calls=%async_computation.3 | async-start | bytes 4423680 | tf_op jit(solution)/shard_map/all_gather | solution.py:267
  892.1 142.7 %all-gather.8.cloned.1.call-start = ((), (), s32[]{:S(2)}) async-start(), calls=%async_computation.4 | async-start | bytes 4423680 | tf_op jit(solution)/shard_map/all_gather | solution.py:275
  915.1 8.0 copy-start.65
  915.1 8.0 copy-start.70
  915.1 8.0 copy-start.69
  915.1 8.1 copy-start.66
  915.1 51.9 %copy-start.49 = (f32[9216]{0:T(1024)S(1)}, f32[9216]{0:T(1024)}, u32[]{:S(2)}) copy-start(f32[9216]{0:T(1024)} %param.18) | copy-start | bytes 110596
  915.2 51.9 %copy-start.62 = (f32[9216]{0:T(1024)S(1)}, f32[9216]{0:T(1024)}, u32[]{:S(2)}) copy-start(f32[9216]{0:T(1024)} %param.19) | copy-start | bytes 110596
  920.4 52.0 %copy-start.29 = (f32[6,96,384]{2,1,0:T(8,128)S(1)}, f32[6,96,384]{2,1,0:T(8,128)}, u32[]{:S(2)}) copy-start(f32[6,96,384]{2,1,0:T(8,128)} %reduce-scatter.2.cloned.1.call-done) | copy-start | bytes 2654212
  972.4 62.4 %copy-start.30 = (f32[6,96,384]{2,1,0:T(8,128)S(1)}, f32[6,96,384]{2,1,0:T(8,128)}, u32[]{:S(2)}) copy-start(f32[6,96,384]{2,1,0:T(8,128)} %param.17) | copy-start | bytes 2654212
  978.4 62.0 %copy-start.43 = (f32[6,96,384]{2,1,0:T(8,128)S(1)}, f32[6,96,384]{2,1,0:T(8,128)}, u32[]{:S(2)}) copy-start(f32[6,96,384]{2,1,0:T(8,128)} %param.21) | copy-start | bytes 2654212
  1034.8 5.5 copy-start.11
  (32 other events, 87.0 us)
Sparse Core Ops, SparseCore 0:
  11.7 105.9 all-gather.3
  630.3 261.7 reduce-scatter.1
  894.2 70.6 all-gather.5
  966.3 68.4 all-gather.7
where the time goes:
time: 1050 us
  waiting for transfers between devices  413 us (39%)
  matrix products  252 us (24%)
  local copies, waits for them, and re-layouts  183 us (17%)
  other arithmetic  144 us (14%)
  blocking collectives  43.2 us (4%)
  between operations  14.8 us (1%)
    reduce_scatter x1, waiting for transfers between devices, per_device(): lax.psum_scatter(grads_laid, ('dp', 'fsdp'), scatter_dimension=1, tiled=T...  262 us
    all_gather x1, waiting for transfers between devices, per_device(): gathered = lax.all_gather(low_shards, ('dp', 'fsdp'), axis=1, tiled=True)  94.6 us
    all_gather x1, waiting for transfers between devices, per_device(): right_whole = lax.all_gather(right_root, 'fsdp', axis=1, tiled=True)  56.4 us
    psum x1, blocking collectives, per_device(): lax.psum((vector_local, square_terms), ('dp', 'fsdp'))  43.2 us
    convert_element_type x1, other arithmetic, attend_backward(): grad_scores = (probs * (grad_probs - inner)).astype(jnp.bfloat16)  42.5 us
    slice x6, local copies, waits for them, and re-layouts, per_device(): used[bounds[index]:bounds[index + 1]]  40.9 us
    dot_general x4, matrix products, block_forward(): jnp.einsum('tik,ijkn->tjn', shaped, grid, preferred_element_type=jnp.floa...  39.3 us
    unnamed x166, local copies, waits for them, and re-layouts  38 us
  transfers between devices with their start and end apart: 4, of which 3 were waited for; matrix products, arithmetic and copies ran while one was open for 5% of the time, Pallas kernels for 0%

commit v1 on v0

v1 whole, which is shorter than its diff:
```python
import functools

import jax
import jax.numpy as jnp
from jax import lax
from jax.experimental import pallas as pl
from jax.experimental.pallas import tpu as pltpu
from jax.sharding import PartitionSpec as P

D = 768
HEADS = 12
HEAD_DIM = 64
FF = 3072
LONGEST = 512

NORM_EPSILON = 1e-05
ROOT_EPSILON = 1e-08
DECAY = 0.5
MATRIX_RATE = 1.5
VECTOR_RATE = 0.1
MASKED = -1e30

BF = jnp.bfloat16
F32 = jnp.float32
PAIR = 2 * HEAD_DIM
TILE = 256
VMEM = 60 * 1024 * 1024

LN1_GAIN, LN1_SHIFT, Q_BIAS, V_BIAS, OUT_BIAS, LN2_GAIN, LN2_SHIFT, PROJ_BIAS, FC_BIAS = range(9)


def nn(left, right):
    return jnp.dot(left, right, preferred_element_type=F32)


def nt(left, right):
    return lax.dot_general(left, right, (((1,), (1,)), ((), ())), preferred_element_type=F32)


def tn(left, right):
    return lax.dot_general(left, right, (((0,), (0,)), ((), ())), preferred_element_type=F32)


def col_sum(values):
    return jnp.sum(values, axis=0, keepdims=True)


def norm_parts(values):
    center = values - jnp.mean(values, axis=-1, keepdims=True)
    spread = jnp.mean(center * center, axis=-1, keepdims=True)
    root = lax.rsqrt(spread + NORM_EPSILON)
    return center * root, root


def norm_back(unit, root, gain, grad):
    scaled = grad * gain
    return root * (
        scaled
        - jnp.mean(scaled, axis=-1, keepdims=True)
        - unit * jnp.mean(scaled * unit, axis=-1, keepdims=True)
    )


def place(weight, blocks, rows, cols):
    width = blocks.shape[-1]
    for row in range(rows):
        for col in range(cols):
            weight[row * width : (row + 1) * width, col * width : (col + 1) * width] = blocks[
                row * cols + col
            ]


def call(kernel, grid, ins, outs, scratch=(), scalars=(), flops=0, name=None):
    spec = pltpu.PrefetchScalarGridSpec(
        num_scalar_prefetch=len(scalars),
        grid=grid,
        in_specs=[pl.BlockSpec(block, index) for _, block, index in ins],
        out_specs=[pl.BlockSpec(block, index) for _, _, block, index in outs],
        scratch_shapes=list(scratch),
    )
    shapes = [jax.ShapeDtypeStruct(shape, dtype) for shape, dtype, _, _ in outs]
    moved = sum(array.size * array.dtype.itemsize for array, _, _ in ins)
    moved += sum(shape.size * shape.dtype.itemsize for shape in shapes)
    return pl.pallas_call(
        kernel,
        grid_spec=spec,
        out_shape=shapes,
        compiler_params=pltpu.CompilerParams(
            dimension_semantics=("arbitrary",) * len(grid), vmem_limit_bytes=VMEM
        ),
        cost_estimate=pl.CostEstimate(flops=flops, bytes_accessed=moved, transcendentals=0),
        name=name,
    )(*scalars, *[array for array, _, _ in ins])


def qkv_kernel(x_ref, vec_ref, blocks_ref, normed_ref, projected_ref, weight):
    @pl.when(pl.program_id(0) == 0)
    def _():
        place(weight, blocks_ref, 2, 6)

    unit, _ = norm_parts(x_ref[...].astype(F32))
    normed = (unit * vec_ref[LN1_GAIN : LN1_GAIN + 1] + vec_ref[LN1_SHIFT : LN1_SHIFT + 1]).astype(
        BF
    )
    normed_ref[...] = normed
    for part in range(3):
        cols = slice(part * D, (part + 1) * D)
        value = nn(normed, weight[:, cols])
        if part != 1:
            row = Q_BIAS if part == 0 else V_BIAS
            value = value + vec_ref[row : row + 1]
        projected_ref[:, cols] = value.astype(BF)


def spans(seq_len):
    out = []
    start = 0
    for first in range(0, seq_len, TILE):
        low = max(0, first - LONGEST)
        out.append((first, low, first + TILE, start))
        start += first + TILE - low
    return out, start


def fill_bias(bias, lengths_ref, row, seq_len, docs):
    for first, low, high, start in spans(seq_len)[0]:
        place_q = lax.broadcasted_iota(jnp.int32, (1, TILE), 1) + first
        begin = jnp.zeros((1, TILE), jnp.int32)
        end = jnp.int32(0)
        for doc in range(docs):
            end = end + lengths_ref[row, doc]
            begin = jnp.where(place_q >= end, end, begin)
        place_k = lax.broadcasted_iota(jnp.int32, (high - low, TILE), 0) + low
        allowed = (place_k >= begin) & (place_k <= place_q)
        bias[start : start + high - low, :] = jnp.where(allowed, 0.0, MASKED)


def head_rows(values, head):
    rows = lax.broadcasted_iota(jnp.int32, values.shape, 0) // HEAD_DIM
    return jnp.where(rows == head, values, jnp.zeros_like(values))


def head_cols(values, head):
    cols = lax.broadcasted_iota(jnp.int32, values.shape, 1) // HEAD_DIM
    return jnp.where(cols == head, values, jnp.zeros_like(values))


def attend_kernel(lengths_ref, q_ref, k_ref, v_ref, out_ref, lse_ref, bias, mixed, *, row, docs):
    seq_len = q_ref.shape[0]

    @pl.when(pl.program_id(0) == 0)
    def _():
        fill_bias(bias, lengths_ref, row, seq_len, docs)

    query_t = (q_ref[...] * BF(HEAD_DIM**-0.5)).T
    value_t = v_ref[...].T
    for head in range(2):
        rows = slice(head * HEAD_DIM, (head + 1) * HEAD_DIM)
        query_h = head_rows(query_t, head)
        for first, low, high, start in spans(seq_len)[0]:
            cols = slice(first, first + TILE)
            scores = nn(k_ref[low:high, :], query_h[:, cols]) + bias[start : start + high - low, :]
            peak = jnp.max(scores, axis=0, keepdims=True)
            weights = jnp.exp(scores - peak)
            total = jnp.sum(weights, axis=0, keepdims=True)
            part = nn(value_t[rows, low:high], weights.astype(BF))
            mixed[rows, cols] = part / total
            lse_ref[0, head : head + 1, cols] = peak + jnp.log(total)
    out_ref[...] = mixed[...].astype(BF).T


def attend_back_kernel(
    lengths_ref,
    q_ref,
    k_ref,
    v_ref,
    out_ref,
    grad_ref,
    lse_ref,
    dq_ref,
    dk_ref,
    dv_ref,
    bias,
    key_sum,
    value_sum,
    query_sum,
    *,
    row,
    docs,
):
    seq_len = q_ref.shape[0]

    @pl.when(pl.program_id(0) == 0)
    def _():
        fill_bias(bias, lengths_ref, row, seq_len, docs)

    query = q_ref[...] * BF(HEAD_DIM**-0.5)
    query_t = query.T
    key_t = k_ref[...].T
    grad = grad_ref[...]
    grad_t = grad.T
    weighted = grad_t.astype(F32) * out_ref[...].T.astype(F32)
    key_sum[...] = jnp.zeros_like(key_sum)
    value_sum[...] = jnp.zeros_like(value_sum)
    for head in range(2):
        rows = slice(head * HEAD_DIM, (head + 1) * HEAD_DIM)
        query_th = head_rows(query_t, head)
        grad_th = head_rows(grad_t, head)
        query_h = head_cols(query, head)
        grad_h = head_cols(grad, head)
        inner = jnp.sum(weighted[rows, :], axis=0, keepdims=True)
        for first, low, high, start in spans(seq_len)[0]:
            cols = slice(first, first + TILE)
            scores = nn(k_ref[low:high, :], query_th[:, cols]) + bias[start : start + high - low, :]
            probs = jnp.exp(scores - lse_ref[0, head : head + 1, cols])
            grad_probs = nn(v_ref[low:high, :], grad_th[:, cols])
            grad_scores = (probs * (grad_probs - inner[:, cols])).astype(BF)
            value_sum[low:high, :] += nn(probs.astype(BF), grad_h[cols, :])
            key_sum[low:high, :] += nn(grad_scores, query_h[cols, :])
            query_sum[rows, cols] = nn(key_t[rows, low:high], grad_scores)
    dq_ref[...] = (query_sum[...] * (HEAD_DIM**-0.5)).astype(BF).T
    dk_ref[...] = key_sum[...].astype(BF)
    dv_ref[...] = value_sum[...].astype(BF)


def out_kernel(att_ref, x_ref, vec_ref, blocks_ref, middle_ref, normed_ref, sums_ref, weight):
    @pl.when(pl.program_id(0) == 0)
    def _():
        place(weight, blocks_ref, 2, 2)
        sums_ref[...] = jnp.zeros_like(sums_ref)

    branch = nn(att_ref[...], weight[...]) + vec_ref[OUT_BIAS : OUT_BIAS + 1]
    middle = x_ref[...].astype(F32) + branch
    middle_ref[...] = middle
    unit, _ = norm_parts(middle)
    normed_ref[...] = (
        unit * vec_ref[LN2_GAIN : LN2_GAIN + 1] + vec_ref[LN2_SHIFT : LN2_SHIFT + 1]
    ).astype(BF)
    sums_ref[0:1] += col_sum(middle * middle)
    sums_ref[1:2] += col_sum(branch * branch)


def mlp_kernel(
    normed_ref,
    cot_ref,
    vec_ref,
    fc_ref,
    proj_ref,
    mlp_ref,
    back_ref,
    dfc_ref,
    dproj_ref,
    bias_ref,
    w_fc,
    w_fc_t,
    w_proj,
    w_proj_t,
    hidden,
    grad_pre,
):
    tile = pl.program_id(0)
    place(w_fc, fc_ref.at[0], 1, 2)
    place(w_fc.at[pl.ds(D // 2, D // 2)], fc_ref.at[1], 1, 2)
    place(w_proj.at[pl.ds(0, D // 2)], proj_ref.at[0], 1, 2)
    place(w_proj.at[pl.ds(D // 2, D // 2)], proj_ref.at[1], 1, 2)
    w_fc_t[...] = w_fc[...].T
    w_proj_t[...] = w_proj[...].T
    bias_row = vec_ref[pl.ds(FC_BIAS + tile, 1)]

    @pl.when(tile == 0)
    def _():
        mlp_ref[...] = jnp.zeros_like(mlp_ref)
        back_ref[...] = jnp.zeros_like(back_ref)

    def chunk(index, total):
        rows = pl.ds(pl.multiple_of(index * TILE, TILE), TILE)
        pre = nn(normed_ref[rows], w_fc[...]) + bias_row
        grad = nn(cot_ref[rows], w_proj_t[...])
        root = 0.7978845608028654
        square = pre * pre
        tanh = jnp.tanh(pre * (root + root * 0.044715 * square))
        half = 0.5 + 0.5 * tanh
        low = (pre * half).astype(BF)
        slope = half + (0.5 * pre) * (1.0 - tanh * tanh) * (root + root * 3.0 * 0.044715 * square)
        back = (grad * slope).astype(BF)
        hidden[rows] = low
        grad_pre[rows] = back
        mlp_ref[rows] += nn(low, w_proj[...])
        back_ref[rows] += nn(back, w_fc_t[...])
        return total + col_sum(back.astype(F32))

    count = normed_ref.shape[0]
    bias_ref[0] = lax.fori_loop(0, count // TILE, chunk, jnp.zeros((1, D), F32))
    half = D // 2
    dproj = tn(hidden[...], cot_ref[...]).astype(BF)
    dfc = tn(normed_ref[...], grad_pre[...]).astype(BF)
    for row in range(2):
        for col in range(2):
            part = (slice(row * half, (row + 1) * half), slice(col * half, (col + 1) * half))
            dproj_ref[row, col] = dproj[part]
            dfc_ref[row, col] = dfc[part]


def middle_kernel(
    middle_ref,
    mlp_ref,
    back_ref,
    cot_ref,
    att_ref,
    vec_ref,
    blocks_ref,
    output_ref,
    grad_ref,
    grad_att_ref,
    dout_ref,
    sums_ref,
    weight,
    branch,
):
    step = pl.program_id(0)

    @pl.when(step == 0)
    def _():
        place(weight, blocks_ref, 2, 2)
        sums_ref[...] = jnp.zeros_like(sums_ref)

    middle = middle_ref[...]
    mlp = mlp_ref[...] + vec_ref[PROJ_BIAS : PROJ_BIAS + 1]
    result = middle + mlp
    output_ref[...] = result.astype(BF)
    cot = cot_ref[...].astype(F32)
    unit, root = norm_parts(middle)
    back = back_ref[...]
    grad = cot + norm_back(unit, root, vec_ref[LN2_GAIN : LN2_GAIN + 1], back)
    grad_ref[...] = grad
    low = grad.astype(BF)
    grad_att_ref[...] = nt(low, weight[...]).astype(BF)
    branch[pl.ds(pl.multiple_of(step * TILE, TILE), TILE)] = low
    sums_ref[0:1] += col_sum(result * result)
    sums_ref[1:2] += col_sum(mlp * mlp)
    sums_ref[2:3] += col_sum(back * unit)
    sums_ref[3:4] += col_sum(back)
    sums_ref[4:5] += col_sum(low.astype(F32))
    sums_ref[5:6] += col_sum(cot)

    @pl.when(step == pl.num_programs(0) - 1)
    def _():
        half = D // 2
        dout = tn(att_ref[...], branch[...]).astype(BF)
        for row in range(2):
            for col in range(2):
                dout_ref[2 * row + col] = dout[
                    row * half : (row + 1) * half, col * half : (col + 1) * half
                ]


def dqkv_kernel(normed_ref, dq_ref, dk_ref, dv_ref, grad_ref, sums_ref):
    half = D // 2
    sums_ref[0:1] = col_sum(dq_ref[...].astype(F32))
    sums_ref[1:2] = col_sum(dv_ref[...].astype(F32))
    for part, ref in enumerate((dq_ref, dk_ref, dv_ref)):
        grad = tn(normed_ref[...], ref[...]).astype(BF)
        for row in range(2):
            for col in range(2):
                grad_ref[row * 6 + part * 2 + col] = grad[
                    row * half : (row + 1) * half, col * half : (col + 1) * half
                ]


def input_kernel(
    x_ref, dq_ref, dk_ref, dv_ref, grad_ref, vec_ref, blocks_ref, out_ref, sums_ref, weight
):
    @pl.when(pl.program_id(0) == 0)
    def _():
        place(weight, blocks_ref, 2, 6)
        sums_ref[...] = jnp.zeros_like(sums_ref)

    back = nt(dq_ref[...], weight[:, :D])
    back += nt(dk_ref[...], weight[:, D : 2 * D])
    back += nt(dv_ref[...], weight[:, 2 * D :])
    unit, root = norm_parts(x_ref[...].astype(F32))
    out_ref[...] = grad_ref[...] + norm_back(unit, root, vec_ref[LN1_GAIN : LN1_GAIN + 1], back)
    sums_ref[0:1] += col_sum(back * unit)
    sums_ref[1:2] += col_sum(back)


def factor_kernel(
    shard_ref,
    grad_ref,
    right_ref,
    matrix_ref,
    left_stat_ref,
    right_stat_ref,
    left_root_ref,
    rows_ref,
    left_ref,
    right_new_ref,
    matrix_new_ref,
    grad_t,
):
    rows = matrix_ref.shape[1]
    grad = grad_ref[0]
    grad_t[...] = grad.T
    own = pl.ds(pl.multiple_of(shard_ref[0] * rows, rows), rows)
    grad_rows = grad_ref[0, own, :]
    rows_ref[0] = grad_rows.astype(F32)
    left_ref[0] = DECAY * left_stat_ref[0] + (1.0 - DECAY) * nn(grad_rows, grad_t[...])
    right_new_ref[0] = DECAY * right_stat_ref[0] + (1.0 - DECAY) * nn(grad_t[own, :], grad)
    half = nn(left_root_ref[0].astype(BF), grad)
    update = nn(half.astype(BF), right_ref[0])
    matrix_new_ref[0] = matrix_ref[0] - MATRIX_RATE * update


def whole(array):
    return (array, array.shape, lambda *_: (0,) * array.ndim)


def tokens_in(array, cols=None):
    return (array, (TILE, cols or array.shape[1]), lambda i, *_: (i, 0))


def out_whole(shape, dtype):
    return (shape, dtype, shape, lambda *_: (0,) * len(shape))


def per_device(
    tokens,
    cotangent,
    doc_lengths,
    block_slot,
    matrices,
    vectors,
    vector_second,
    left_stat,
    right_stat,
    left_root,
    right_root,
):
    dp_count = lax.axis_size("dp")
    fsdp_count = lax.axis_size("fsdp")
    own_blocks, own_rows, width = matrices.shape
    blocks = own_blocks * dp_count
    slot_place = block_slot % own_blocks * dp_count + block_slot // own_blocks
    low_shards = matrices.astype(BF)
    gathered = lax.all_gather(low_shards, ("dp", "fsdp"), axis=1, tiled=True)
    used = jnp.take(gathered.reshape(blocks, width, width), slot_place, axis=0)
    right_whole = lax.all_gather(right_root.astype(BF), "fsdp", axis=1, tiled=True)

    vec = vectors.reshape(-1, D)
    count = tokens.shape[0]
    rows_here, docs = doc_lengths.shape
    seq_len = count // rows_here
    steps = count // TILE
    weight_scratch = [pltpu.VMEM((D, 3 * D), BF)]
    small_scratch = [pltpu.VMEM((D, D), BF)]
    qkv_in = (used, (12, width, width), lambda *_: (0, 0, 0))
    out_in = (used, (4, width, width), lambda *_: (3, 0, 0))

    normed1, projected = call(
        qkv_kernel,
        (steps,),
        [tokens_in(tokens), whole(vec), qkv_in],
        [
            ((count, D), BF, (TILE, D), lambda i: (i, 0)),
            ((count, 3 * D), BF, (TILE, 3 * D), lambda i: (i, 0)),
        ],
        weight_scratch,
        flops=2 * count * D * 3 * D,
        name="qkv",
    )

    pairs = HEADS // 2
    bias_rows = spans(seq_len)[1]

    def pair_in(array, row, offset):
        return (array, (seq_len, PAIR), lambda p, *_: (row, offset + p))

    attended, lses = [], []
    for row in range(rows_here):
        one, lse = call(
            functools.partial(attend_kernel, row=row, docs=docs),
            (pairs,),
            [pair_in(projected, row, part * pairs) for part in range(3)],
            [
                ((seq_len, D), BF, (seq_len, PAIR), lambda p, *_: (0, p)),
                ((pairs, 2, seq_len), F32, (1, 2, seq_len), lambda p, *_: (p, 0, 0)),
            ],
            [pltpu.VMEM((bias_rows, TILE), F32), pltpu.VMEM((PAIR, seq_len), F32)],
            scalars=[doc_lengths],
            flops=8 * seq_len * seq_len * D,
            name="attend",
        )
        attended.append(one)
        lses.append(lse)
    attended = attended[0] if rows_here == 1 else jnp.concatenate(attended, axis=0)

    middle, normed2, sums_mid = call(
        out_kernel,
        (steps,),
        [tokens_in(attended), tokens_in(tokens), whole(vec), out_in],
        [
            ((count, D), F32, (TILE, D), lambda i: (i, 0)),
            ((count, D), BF, (TILE, D), lambda i: (i, 0)),
            out_whole((8, D), F32),
        ],
        small_scratch,
        flops=2 * count * D * D,
        name="attn_out",
    )

    ff_tiles = FF // D
    fc_view = used.reshape(6, 8, width, width)
    proj_view = used.reshape(24, 2, width, width)
    mlp, back2, dfc, dproj, fc_bias_grad = call(
        mlp_kernel,
        (ff_tiles,),
        [
            whole(normed2),
            whole(cotangent),
            whole(vec),
            (fc_view, (2, 2, width, width), lambda t: (1, t, 0, 0)),
            (proj_view, (2, 2, width, width), lambda t: (8 + t, 0, 0, 0)),
        ],
        [
            out_whole((count, D), F32),
            out_whole((count, D), F32),
            ((2, 8, width, width), BF, (2, 2, width, width), lambda t: (0, t, 0, 0)),
            ((8, 2, width, width), BF, (2, 2, width, width), lambda t: (t, 0, 0, 0)),
            ((ff_tiles, 1, D), F32, (1, 1, D), lambda t: (t, 0, 0)),
        ],
        [pltpu.VMEM((D, D), BF)] * 4 + [pltpu.VMEM((count, D), BF)] * 2,
        flops=12 * count * D * FF,
        name="mlp",
    )

    output, grad_middle, grad_attended, dout, sums_back = call(
        middle_kernel,
        (steps,),
        [
            tokens_in(middle),
            tokens_in(mlp),
            tokens_in(back2),
            tokens_in(cotangent),
            whole(attended),
            whole(vec),
            out_in,
        ],
        [
            ((count, D), BF, (TILE, D), lambda i: (i, 0)),
            ((count, D), F32, (TILE, D), lambda i: (i, 0)),
            ((count, D), BF, (TILE, D), lambda i: (i, 0)),
            out_whole((4, width, width), BF),
            out_whole((8, D), F32),
        ],
        small_scratch + [pltpu.VMEM((count, D), BF)],
        flops=4 * count * D * D,
        name="middle_back",
    )

    query_grads, key_grads, value_grads = [], [], []
    for row in range(rows_here):
        grads = call(
            functools.partial(attend_back_kernel, row=row, docs=docs),
            (pairs,),
            [pair_in(projected, row, part * pairs) for part in range(3)]
            + [
                pair_in(attended, row, 0),
                pair_in(grad_attended, row, 0),
                (lses[row], (1, 2, seq_len), lambda p, *_: (p, 0, 0)),
            ],
            [((seq_len, D), BF, (seq_len, PAIR), lambda p, *_: (0, p))] * 3,
            [
                pltpu.VMEM((bias_rows, TILE), F32),
                pltpu.VMEM((seq_len, PAIR), F32),
                pltpu.VMEM((seq_len, PAIR), F32),
                pltpu.VMEM((PAIR, seq_len), F32),
            ],
            scalars=[doc_lengths],
            flops=20 * seq_len * seq_len * D,
            name="attend_back",
        )
        for held, one in zip((query_grads, key_grads, value_grads), grads):
            held.append(one)
    dq, dk, dv = [
        held[0] if rows_here == 1 else jnp.concatenate(held, axis=0)
        for held in (query_grads, key_grads, value_grads)
    ]

    dqkv, sums_qkv = call(
        dqkv_kernel,
        (1,),
        [whole(normed1), whole(dq), whole(dk), whole(dv)],
        [out_whole((12, width, width), BF), out_whole((8, D), F32)],
        flops=2 * count * D * 3 * D,
        name="qkv_weight_back",
    )
    x_grad, sums_in = call(
        input_kernel,
        (steps,),
        [
            tokens_in(tokens),
            tokens_in(dq),
            tokens_in(dk),
            tokens_in(dv),
            tokens_in(grad_middle),
            whole(vec),
            qkv_in,
        ],
        [((count, D), F32, (TILE, D), lambda i: (i, 0)), out_whole((8, D), F32)],
        weight_scratch,
        flops=2 * count * D * 3 * D,
        name="input_back",
    )

    vector_local = jnp.concatenate(
        [
            sums_in[0],
            sums_in[1],
            sums_qkv[0],
            sums_qkv[1],
            sums_back[4],
            sums_back[2],
            sums_back[3],
            sums_back[5],
            fc_bias_grad.reshape(-1),
        ]
    )
    square_terms = jnp.stack(
        [jnp.sum(sums_mid[0]), jnp.sum(sums_back[0]), jnp.sum(sums_mid[1]), jnp.sum(sums_back[1])]
    )
    vector_grad, square_sums = lax.psum((vector_local, square_terms), ("dp", "fsdp"))

    grads_used = jnp.concatenate(
        [dqkv, dout, dfc.reshape(16, width, width), dproj.reshape(16, width, width)], axis=0
    )
    grads_laid = jnp.take(grads_used, jnp.argsort(slot_place), axis=0).reshape(
        own_blocks, dp_count * width, width
    )
    grad_rows = lax.psum_scatter(grads_laid, ("dp", "fsdp"), scatter_dimension=1, tiled=True)
    grad_whole = lax.all_gather(grad_rows, "fsdp", axis=1, tiled=True)

    shard = lax.axis_index("fsdp").astype(jnp.int32).reshape(1)

    def block_in(array):
        return (array, (1,) + array.shape[1:], lambda b, *_: (b, 0, 0))

    matrix_grad, left_new, right_new, matrix_new = call(
        factor_kernel,
        (own_blocks,),
        [
            block_in(a)
            for a in (grad_whole, right_whole, matrices, left_stat, right_stat, left_root)
        ],
        [(matrices.shape, F32, (1, own_rows, width), lambda b, *_: (b, 0, 0))] * 4,
        [pltpu.VMEM((width, width), BF)],
        scalars=[shard],
        flops=8 * own_blocks * own_rows * width * width,
        name="factor",
    )

    residual_scale = jnp.sqrt(square_sums / (count * dp_count * fsdp_count * D))
    second_new = DECAY * vector_second + (1.0 - DECAY) * vector_grad * vector_grad
    vector_new = vectors - VECTOR_RATE * vector_grad / (jnp.sqrt(second_new) + ROOT_EPSILON)
    return (
        output,
        x_grad,
        matrix_grad,
        left_new,
        right_new,
        matrix_new,
        vector_grad,
        second_new,
        vector_new,
        residual_scale,
    )


def solution(mesh):
    tokens = P(("dp", "fsdp"), None)
    stored = P("dp", "fsdp", None)
    return jax.shard_map(
        per_device,
        mesh=mesh,
        in_specs=(tokens, tokens, tokens, P(), stored, P(), P()) + (stored,) * 4,
        out_specs=(tokens, tokens) + (stored,) * 4 + (P(),) * 4,
        check_vma=False,
    )
```

time: 1050 us -> 545 us (0.52)
  matrix products: 252 us -> 0 us
  local copies, waits for them, and re-layouts: 183 us -> 28.9 us
  waiting for transfers between devices: 413 us -> 265 us
  Pallas kernels: 0 us -> 143 us
  other arithmetic: 144 us -> 50.6 us
    dot_general x28 -> x0, matrix products: 252 us -> none  [the longest x4 39.3 us: block_forward(): jnp.einsum('tik,ijkn->tjn', shaped, grid, preferred_element_type=jnp.floa...]
    pallas_call x0 -> x9, Pallas kernels: none -> 143 us  [call(): pl.pallas_call(kernel, grid_spec=spec, out_shape=shapes, compiler_params=...]
    reduce_scatter x1, waiting for transfers between devices: 262 us -> 161 us  [per_device(): lax.psum_scatter(grads_laid, ('dp', 'fsdp'), scatter_dimension=1, tiled=T...]
    all_gather x1, waiting for transfers between devices: 56.4 us -> 0.01 us  [per_device(): lax.all_gather(right_root.astype(BF), 'fsdp', axis=1, tiled=True)]
    slice x19 -> x2, local copies, waits for them, and re-layouts: 55.4 us -> 1.67 us  [the longest x1 0.84 us: per_device(): sums_qkv[1]]
    convert_element_type x4 -> x2, other arithmetic: 50.1 us -> 2.79 us  [the longest x1 1.98 us: per_device(): low_shards = matrices.astype(BF)]
    unnamed x166 -> x22, local copies, waits for them, and re-layouts: 38 us -> 1.16 us
    reduce_sum x12 -> x2, other arithmetic: 35.7 us -> 2.03 us  [the longest x1 1.43 us: per_device(): jnp.sum(sums_mid[0])]
  transfers between devices with their start and end apart: 4 -> 4, of which waited for: 3 -> 2; matrix products, arithmetic and copies ran while one was open for 5% -> 2% of each run, Pallas kernels for 0% -> 2%
where the time goes in v1:
time: 545 us; the launch traced here: 544 us
  waiting for transfers between devices  265 us (49%)
  Pallas kernels  143 us (26%)
  other arithmetic  50.6 us (9%)
  blocking collectives  40.4 us (7%)
  local copies, waits for them, and re-layouts  28.9 us (5%)
  between operations  15.7 us (3%)
    reduce_scatter x1, waiting for transfers between devices, per_device(): lax.psum_scatter(grads_laid, ('dp', 'fsdp'), scatter_dimension=1, tiled=T...  161 us
    pallas_call x9, Pallas kernels, call(): pl.pallas_call(kernel, grid_spec=spec, out_shape=shapes, compiler_params=...  143 us
    all_gather x1, waiting for transfers between devices, per_device(): gathered = lax.all_gather(low_shards, ('dp', 'fsdp'), axis=1, tiled=True)  104 us
    psum x1, blocking collectives, per_device(): lax.psum((vector_local, square_terms), ('dp', 'fsdp'))  40.4 us
    select_n x2, other arithmetic, per_device(): jnp.take(grads_used, jnp.argsort(slot_place), axis=0)  13.2 us
    select_n x2, other arithmetic, per_device(): used = jnp.take(gathered.reshape(blocks, width, width), slot_place, axis=0)  13.2 us
    concatenate x1, other arithmetic, per_device(): jnp.concatenate([dqkv, dout, dfc.reshape(16, width, width), dproj.reshape...  12.8 us
    gather x1, local copies, waits for them, and re-layouts, per_device(): used = jnp.take(gathered.reshape(blocks, width, width), slot_place, axis=0)  12.4 us
  transfers between devices with their start and end apart: 4, of which 2 were waited for; matrix products, arithmetic and copies ran while one was open for 2% of the time, Pallas kernels for 2%

profile of v1, /device:TPU:0, one launch (start us, length us, event | category | flops | bytes accessed | tf_op | source)
XLA Modules:
  0.0 543.8 jit_solution(10872697790985756452)
XLA Ops:
  8.0 0.0 all-gather.4.cloned.1.call-start
  8.1 2.0 convert_element_type.6
  10.0 0.0 all-gather.4.cloned.1.call-update
  10.1 0.0 reduce-scatter.2.cloned.1.call-start
  10.1 1.4 reshape.52.vec_ref
  11.5 0.7 compare_and_fusion.1
  12.2 2.0 sort.17
  14.3 104.2 %all-gather.4.cloned.1.call-done = bf16[6,3072,384]{2,1,0:T(8,128)(2,1)} async-done(((bf16[6,96,384]{2,1,0:T(8,128)(2,1)}), bf16[6,3072,384]{2,1,0:T(8,128)(2,1)}) %all-gather.4.cloned.1.call-update) | async-done | bytes 14155792 | tf_op jit(solution)/shard_map/all_gather | solution.py:445
  118.5 12.4 %gather_fusion = bf16[48,384,384]{2,1,0:T(8,128)(2,1)} fusion(bf16[48,384,384]{2,1,0:T(8,128)(2,1)} %bitcast.15, s32[1024]{0:T(1024)S(1)} %pad_clamp_fusion.1), kind=kCustom, calls=%fused_computation.clone | custom fusion | bytes 28311744 | tf_op jit(solution)/shard_map/jit(_take)/gather | solution.py:446
  130.9 13.2 %broadcast_select_fusion.1.blocks_ref = bf16[48,384,384]{2,1,0:T(8,128)(2,1)} fusion(bf16[48,384,384]{2,1,0:T(8,128)(2,1)} %gather_fusion, pred[48]{0:T(512)(128)(4,1)S(1)} %get-tuple-element.85), kind=kLoop, calls=%fused_computation.4 | loop fusion | flops 7077888 | bytes 28311600 | tf_op jit(solution)/shard_map/jit(_take)/select_n | solution.py:446
  144.1 8.8 %qkv.1 = (bf16[1024,768]{1,0:T(8,128)(2,1)}, bf16[1024,2304]{1,0:T(8,128)(2,1)}) custom-call(bf16[1024,768]{1,0:T(8,128)(2,1)} %x_ref.5, f32[12,768]{1,0:T(8,128)} %reshape.52.vec_ref, bf16[48,384,384]{2,1,0:T(8,128)(2,1)} %broadcast_select_fusion.1.blocks_ref), custom_call_target="tpu_custom_call" | custom-call | flops 3623878656 | bytes 22056960 | tf_op jit(solution)/shard_map/qkv/pallas_call | solution.py:84
  152.8 24.2 %attend.1 = (bf16[1024,768]{1,0:T(8,128)(2,1)}, f32[6,2,1024]{2,1,0:T(2,128)}) custom-call(s32[1,8]{1,0:T(1,128)} %lengths_ref.3, bf16[1024,2304]{1,0:T(8,128)(2,1)} %get-tuple-element.40.q_ref.k_ref.v_ref, bf16[1024,2304]{1,0:T(8,128)(2,1)} %get-tuple-element.40.q_ref.k_ref.v_ref, bf16[1024,2304]{1,0:T(8,128)(2,1)} %get-tuple-element.40.q_ref.k_ref.v_ref), custom_call_target="tpu_custom_call" | custom-call | flops 6442450944 | bytes 15777792 | tf_op jit(solution)/shard_map/attend/pallas_call | solution.py:84
  177.1 6.2 %attn_out.1 = (f32[1024,768]{1,0:T(8,128)}, bf16[1024,768]{1,0:T(8,128)(2,1)}, f32[8,768]{1,0:T(8,128)}) custom-call(bf16[1024,768]{1,0:T(8,128)(2,1)} %get-tuple-element.41.att_ref.out_ref, bf16[1024,768]{1,0:T(8,128)(2,1)} %x_ref.5, f32[12,768]{1,0:T(8,128)} %reshape.52.vec_ref, bf16[48,384,384]{2,1,0:T(8,128)(2,1)} %broadcast_select_fusion.1.blocks_ref), custom_call_target="tpu_custom_call" | custom-call | flops 1207959552 | bytes 22081536 | tf_op jit(solution)/shard_map/attn_out/pallas_call | solution.py:84
  183.2 42.2 %mlp.1 = (f32[1024,768]{1,0:T(8,128)}, f32[1024,768]{1,0:T(8,128)}, bf16[2,8,384,384]{3,2,1,0:T(8,128)(2,1)}, bf16[8,2,384,384]{3,2,1,0:T(8,128)(2,1)}, f32[4,1,768]{2,1,0:T(1,128)}) custom-call(bf16[1024,768]{1,0:T(8,128)(2,1)} %get-tuple-element.43.normed_ref, bf16[1024,768]{1,0:T(8,128)(2,1)} %cot_ref.3, f32[12,768]{1,0:T(8,128)} %reshape.52.vec_ref, ...), custom_call_target="tpu_custom_call" | custom-call | flops 28991029248 | bytes 47235072 | tf_op jit(solution)/shard_map/mlp/pallas_call | solution.py:84
  225.4 12.4 %middle_back.1 = (bf16[1024,768]{1,0:T(8,128)(2,1)}, f32[1024,768]{1,0:T(8,128)}, bf16[1024,768]{1,0:T(8,128)(2,1)}, bf16[4,384,384]{2,1,0:T(8,128)(2,1)}, f32[8,768]{1,0:T(8,128)}) custom-call(f32[1024,768]{1,0:T(8,128)} %get-tuple-element.42.middle_ref, f32[1024,768]{1,0:T(8,128)} %get-tuple-element.44.mlp_ref, f32[1024,768]{1,0:T(8,128)} %get-tuple-element.45.back_ref, ...), custom_call_target="tpu_custom_call" | custom-call | flops 2415919104 | bytes 34271232 | tf_op jit(solution)/shard_map/middle_back/pallas_call | solution.py:84
  237.7 22.7 %attend_back.1 = (bf16[1024,768]{1,0:T(8,128)(2,1)}, bf16[1024,768]{1,0:T(8,128)(2,1)}, bf16[1024,768]{1,0:T(8,128)(2,1)}) custom-call(s32[1,8]{1,0:T(1,128)} %lengths_ref.3, bf16[1024,2304]{1,0:T(8,128)(2,1)} %get-tuple-element.40.q_ref.k_ref.v_ref, bf16[1024,2304]{1,0:T(8,128)(2,1)} %get-tuple-element.40.q_ref.k_ref.v_ref, ...), custom_call_target="tpu_custom_call" | custom-call | flops 16106127360 | bytes 22069248 | tf_op jit(solution)/shard_map/attend_back/pallas_call | solution.py:84
  260.4 0.0 copy-start
  260.4 8.6 %qkv_weight_back.1 = (bf16[12,384,384]{2,1,0:T(8,128)(2,1)}, f32[8,768]{1,0:T(8,128)}) custom-call(bf16[1024,768]{1,0:T(8,128)(2,1)} %get-tuple-element.54.normed_ref, bf16[1024,768]{1,0:T(8,128)(2,1)} %get-tuple-element.49.dq_ref, bf16[1024,768]{1,0:T(8,128)(2,1)} %get-tuple-element.50.dk_ref, bf16[1024,768]{1,0:T(8,128)(2,1)} %get-tuple-element.51.dv_ref), custom_call_target="tpu_custom_call" | custom-call | flops 3623878656 | bytes 9854976 | tf_op jit(solution)/shard_map/qkv_weight_back/pallas_call | solution.py:84
  269.0 0.0 copy-done
  269.0 12.8 %pad_maximum_fusion = bf16[48,384,384]{2,1,0:T(8,128)(2,1)} fusion(bf16[16,384,384]{2,1,0:T(8,128)(2,1)} %bitcast.17, bf16[16,384,384]{2,1,0:T(8,128)(2,1)} %bitcast.16, bf16[4,384,384]{2,1,0:T(8,128)(2,1)S(1)} %copy-done, bf16[12,384,384]{2,1,0:T(8,128)(2,1)} %get-tuple-element.55), kind=kLoop, calls=%fused_computation.2 | loop fusion | flops 21233664 | bytes 28311552 | tf_op jit(solution)/shard_map/concatenate | solution.py:633
  281.8 12.2 %gather_fusion.1 = bf16[48,384,384]{2,1,0:T(8,128)(2,1)} fusion(bf16[48,384,384]{2,1,0:T(8,128)(2,1)} %pad_maximum_fusion, s32[1024]{0:T(1024)S(1)} %pad_clamp_fusion), kind=kCustom, calls=%fused_computation.1.clone | custom fusion | bytes 28311744 | tf_op jit(solution)/shard_map/jit(_take)/gather | solution.py:636
  294.0 13.2 %broadcast_select_fusion = bf16[48,384,384]{2,1,0:T(8,128)(2,1)} fusion(bf16[48,384,384]{2,1,0:T(8,128)(2,1)} %gather_fusion.1, pred[48]{0:T(512)(128)(4,1)S(1)} %compare_and_fusion), kind=kLoop, calls=%fused_computation.3 | loop fusion | flops 7077888 | bytes 28311600 | tf_op jit(solution)/shard_map/jit(_take)/select_n | solution.py:636
  307.3 0.0 copy-start.1
  307.3 0.0 copy-start.5
  307.3 0.0 reduce-scatter.2.cloned.1.call-update
  307.3 0.0 all-gather.8.cloned.1.call-start
  307.3 1.1 copy-done.1
  308.4 0.8 convert_element_type.7
  309.2 0.0 all-gather.8.cloned.1.call-update
  309.3 0.0 all-gather.6.cloned.1.call-start
  309.3 160.7 %reduce-scatter.2.cloned.1.call-done = bf16[6,96,384]{2,1,0:T(8,128)(2,1)} async-done(((bf16[6,3072,384]{2,1,0:T(8,128)(2,1)}), bf16[6,96,384]{2,1,0:T(8,128)(2,1)}) %reduce-scatter.2.cloned.1.call-update) | async-done | bytes 442384 | tf_op jit(solution)/shard_map/reduce_scatter | solution.py:639
  470.0 0.0 all-gather.6.cloned.1.call-update
  470.1 1.4 slice_reduce_fusion.3
  471.5 0.0 copy-done.5
  471.5 0.6 slice_reduce_fusion.2
  472.1 2.7 pad_maximum_fusion.1
  474.8 10.9 %input_back.1 = (f32[1024,768]{1,0:T(8,128)}, f32[8,768]{1,0:T(8,128)}) custom-call(bf16[1024,768]{1,0:T(8,128)(2,1)} %x_ref.5, bf16[1024,768]{1,0:T(8,128)(2,1)} %get-tuple-element.49.dq_ref, bf16[1024,768]{1,0:T(8,128)(2,1)} %get-tuple-element.50.dk_ref, bf16[1024,768]{1,0:T(8,128)(2,1)} %get-tuple-element.51.dv_ref, ...), custom_call_target="tpu_custom_call" | custom-call | flops 3623878656 | bytes 26800128 | tf_op jit(solution)/shard_map/input_back/pallas_call | solution.py:84
  485.7 0.8 slice_reduce_fusion.10
  486.6 0.8 slice_reduce_fusion.8
  487.5 0.0 copy-done.6
  487.5 40.4 %all-reduce = (f32[9216]{0:T(1024)S(1)}, f32[4]{0:T(128)S(1)}) all-reduce(f32[9216]{0:T(1024)S(1)} %constant_dynamic-update-slice_fusion, f32[4]{0:T(128)S(1)} %pad_maximum_fusion.1), channel_id=1, replica_groups=mesh['dp'=8,'fsdp'=4] {'dp','fsdp'}, use_global_device_ids=true, to_apply=%region_2.4 | all-reduce | flops 9220 | bytes 73760 | tf_op jit(solution)/shard_map/psum | solution.py:631
  528.0 0.0 copy-start.4
  528.0 0.5 multiply_sqrt_fusion
  528.5 0.0 copy-done.2
  528.5 0.0 copy-done.3
  528.5 0.6 divide_subtract_fusion
  529.2 7.2 %factor.1 = (f32[6,96,384]{2,1,0:T(8,128)}, f32[6,96,384]{2,1,0:T(8,128)}, f32[6,96,384]{2,1,0:T(8,128)}, f32[6,96,384]{2,1,0:T(8,128)}) custom-call(s32[1]{0:T(128)} %bitcast.3.shard_ref, bf16[6,384,384]{2,1,0:T(8,128)(2,1)} %all-gather.6.cloned.1.call-done.grad_ref, bf16[6,384,384]{2,1,0:T(8,128)(2,1)} %all-gather.8.cloned.1.call-done.right_ref, ...), custom_call_target="tpu_custom_call" | custom-call | flops 679477248 | bytes 10616832 | tf_op jit(solution)/shard_map/factor/pallas_call | solution.py:84
  536.3 0.0 copy-done.4
  (21 shorter events, 0.1 us)
Async XLA Ops:
  8.0 110.5 %all-gather.4.cloned.1.call-start = ((), (), s32[]{:S(2)}) async-start(), calls=%async_computation.1 | async-start | bytes 14598144 | tf_op jit(solution)/shard_map/all_gather | solution.py:445
  10.1 460.0 %reduce-scatter.2.cloned.1.call-start = ((), (), s32[]{:S(2)}) async-start(), calls=%async_computation.2 | async-start | bytes 14598144 | tf_op jit(solution)/shard_map/reduce_scatter | solution.py:639
  260.4 8.6 %copy-start = (bf16[4,384,384]{2,1,0:T(8,128)(2,1)S(1)}, bf16[4,384,384]{2,1,0:T(8,128)(2,1)}, u32[]{:S(2)}) copy-start(bf16[4,384,384]{2,1,0:T(8,128)(2,1)} %get-tuple-element.56) | copy-start | bytes 3538948
  307.3 1.2 copy-start.1
  307.3 164.2 %copy-start.5 = (f32[8,768]{1,0:T(8,128)S(1)}, f32[8,768]{1,0:T(8,128)}, u32[]{:S(2)}) copy-start(f32[8,768]{1,0:T(8,128)} %get-tuple-element.66) | copy-start | bytes 73732
  307.3 221.9 %all-gather.8.cloned.1.call-start = ((), (), s32[]{:S(2)}) async-start(), calls=%async_computation.4 | async-start | bytes 2211840 | tf_op jit(solution)/shard_map/all_gather | solution.py:447
  309.3 219.9 %all-gather.6.cloned.1.call-start = ((), (), s32[]{:S(2)}) async-start(), calls=%async_computation.3 | async-start | bytes 2211840 | tf_op jit(solution)/shard_map/all_gather | solution.py:640
  474.8 12.7 %copy-start.6 = (f32[4,1,768]{2,1,0:T(1,128)S(1)}, f32[4,1,768]{2,1,0:T(1,128)}, u32[]{:S(2)}) copy-start(f32[4,1,768]{2,1,0:T(1,128)} %get-tuple-element.67) | copy-start | bytes 36868
  474.8 53.7 %copy-start.2 = (f32[9216]{0:T(1024)S(1)}, f32[9216]{0:T(1024)}, u32[]{:S(2)}) copy-start(f32[9216]{0:T(1024)} %param.18) | copy-start | bytes 110596
  474.8 53.7 %copy-start.3 = (f32[9216]{0:T(1024)S(1)}, f32[9216]{0:T(1024)}, u32[]{:S(2)}) copy-start(f32[9216]{0:T(1024)} %param.19) | copy-start | bytes 110596
  528.0 8.4 %copy-start.4 = (f32[9216]{0:T(1024)}, f32[9216]{0:T(1024)S(1)}, u32[]{:S(2)}) copy-start(f32[9216]{0:T(1024)S(1)} %get-tuple-element.81) | copy-start | bytes 110596
Sparse Core Ops, SparseCore 0:
  12.5 105.9 all-gather.3
  307.4 162.5 reduce-scatter.1
Sparse Core Ops, SparseCore 1:
  309.9 38.3 all-gather.7
  470.1 39.3 all-gather.5

commit v2 on v1

--- a/solution.py
+++ b/solution.py
@@ -25,6 +25,7 @@
 PAIR = 2 * HEAD_DIM
 TILE = 256
 VMEM = 60 * 1024 * 1024
+FIRST_TILES = 2
 
 LN1_GAIN, LN1_SHIFT, Q_BIAS, V_BIAS, OUT_BIAS, LN2_GAIN, LN2_SHIFT, PROJ_BIAS, FC_BIAS = range(9)
 
@@ -62,41 +63,136 @@
 
 
 def place(weight, blocks, rows, cols):
-    width = blocks.shape[-1]
+    width = blocks[0].shape[-1]
     for row in range(rows):
         for col in range(cols):
             weight[row * width : (row + 1) * width, col * width : (col + 1) * width] = blocks[
                 row * cols + col
-            ]
-
-
-def call(kernel, grid, ins, outs, scratch=(), scalars=(), flops=0, name=None):
+            ][0]
+
+
+def call(kernel, grid, ins, outs, scratch=(), scalars=(), ties=(), name=None):
+    first = len(scalars) + len(ins)
+
+    def body(*refs):
+        kernel(*refs[:first], *refs[first + len(ties) :])
+
     spec = pltpu.PrefetchScalarGridSpec(
         num_scalar_prefetch=len(scalars),
         grid=grid,
-        in_specs=[pl.BlockSpec(block, index) for _, block, index in ins],
+        in_specs=[pl.BlockSpec(block, index) for _, block, index in ins]
+        + [pl.BlockSpec(memory_space=pl.ANY)] * len(ties),
         out_specs=[pl.BlockSpec(block, index) for _, _, block, index in outs],
         scratch_shapes=list(scratch),
     )
-    shapes = [jax.ShapeDtypeStruct(shape, dtype) for shape, dtype, _, _ in outs]
-    moved = sum(array.size * array.dtype.itemsize for array, _, _ in ins)
-    moved += sum(shape.size * shape.dtype.itemsize for shape in shapes)
     return pl.pallas_call(
-        kernel,
+        body,
         grid_spec=spec,
-        out_shape=shapes,
+        out_shape=[jax.ShapeDtypeStruct(shape, dtype) for shape, dtype, _, _ in outs],
         compiler_params=pltpu.CompilerParams(
             dimension_semantics=("arbitrary",) * len(grid), vmem_limit_bytes=VMEM
         ),
-        cost_estimate=pl.CostEstimate(flops=flops, bytes_accessed=moved, transcendentals=0),
+        cost_estimate=pl.CostEstimate(flops=1024, bytes_accessed=1024, transcendentals=0),
         name=name,
-    )(*scalars, *[array for array, _, _ in ins])
-
-
-def qkv_kernel(x_ref, vec_ref, blocks_ref, normed_ref, projected_ref, weight):
+    )(*scalars, *[array for array, _, _ in ins], *ties)
+
+
+def whole(array):
+    return (array, array.shape, lambda *_: (0,) * array.ndim)
+
+
+def tokens_in(array, cols=None):
+    return (array, (TILE, cols or array.shape[1]), lambda i, *_: (i, 0))
+
+
+def out_whole(shape, dtype):
+    return (shape, dtype, shape, lambda *_: (0,) * len(shape))
+
+
+def plane_sum_kernel(half_ref, *refs):
+    half = len(refs) // 2
+    for parts, out in zip(refs[:half], refs[half:]):
+        total = parts[0].astype(F32)
+        for part in range(1, parts.shape[0]):
+            total = total + parts[part].astype(F32)
+        out[...] = total.astype(BF)
+
+
+def plane_sum(parts, half, ties, name):
+    count, blocks, height, width = parts.shape
+    size = blocks // 2
+
+    def group(offset):
+        return (parts, (count, size, height, width), lambda i, at: (0, at[0] ^ offset, 0, 0))
+
+    return call(
+        plane_sum_kernel,
+        (1,),
+        [group(0), group(1)],
+        [out_whole((size, height, width), BF)] * 2,
+        scalars=[half],
+        ties=ties,
+        name=name,
+    )
+
+
+def add_kernel(left_ref, right_ref, out_ref):
+    out_ref[...] = (left_ref[...].astype(F32) + right_ref[...].astype(F32)).astype(BF)
+
+
+def add_up(left, right, ties, name):
+    return call(
+        add_kernel,
+        (1,),
+        [whole(left), whole(right)],
+        [out_whole(left.shape, BF)],
+        ties=ties,
+        name=name,
+    )[0]
+
+
+def line_half(halves, ties, name):
+    return add_up(halves[0], across_fsdp(halves[1], 1), ties, name)
+
+
+def line_rest(total, ties, name):
+    offset = 3
+    while offset <= lax.axis_size("fsdp"):
+        total = add_up(total, across_fsdp(total, offset), ties, name)
+        offset = 2 * offset - 1
+    return total
+
+
+def line_spread(total):
+    return [total, across_fsdp(total, 1)]
+
+
+def pack_kernel(in_ref, qkv_ref, back_ref, mid_ref, *refs):
+    fc_refs, out_ref = refs[:-1], refs[-1]
+    out_ref[0:2] = in_ref[0:2]
+    out_ref[2:4] = qkv_ref[0:2]
+    out_ref[4:5] = back_ref[4:5]
+    out_ref[5:7] = back_ref[2:4]
+    out_ref[7:8] = back_ref[5:6]
+    row = 8
+    for ref in fc_refs:
+        for tile in range(ref.shape[0]):
+            out_ref[row : row + 1] = ref[tile]
+            row += 1
+    lanes = lax.broadcasted_iota(jnp.int32, (1, D), 1)
+    line = jnp.zeros((1, D), F32)
+    for lane, value in enumerate((mid_ref[0:1], back_ref[0:1], mid_ref[1:2], back_ref[1:2])):
+        line = jnp.where(lanes == lane, jnp.sum(value), line)
+    out_ref[row : row + 1] = line
+    out_ref[row + 1 :] = jnp.zeros_like(out_ref[row + 1 :])
+
+
+def qkv_kernel(place_ref, x_ref, vec_ref, *refs):
+    blocks, (normed_ref, projected_ref, weight) = refs[:12], refs[12:]
+
     @pl.when(pl.program_id(0) == 0)
     def _():
-        place(weight, blocks_ref, 2, 6)
+        place(weight, blocks, 2, 6)
 
     unit, _ = norm_parts(x_ref[...].astype(F32))
     normed = (unit * vec_ref[LN1_GAIN : LN1_GAIN + 1] + vec_ref[LN1_SHIFT : LN1_SHIFT + 1]).astype(
@@ -223,10 +319,12 @@
     dv_ref[...] = value_sum[...].astype(BF)
 
 
-def out_kernel(att_ref, x_ref, vec_ref, blocks_ref, middle_ref, normed_ref, sums_ref, weight):
+def out_kernel(place_ref, att_ref, x_ref, vec_ref, *refs):
+    blocks, (middle_ref, normed_ref, sums_ref, weight) = refs[:4], refs[4:]
+
     @pl.when(pl.program_id(0) == 0)
     def _():
-        place(weight, blocks_ref, 2, 2)
+        place(weight, blocks, 2, 2)
         sums_ref[...] = jnp.zeros_like(sums_ref)
 
     branch = nn(att_ref[...], weight[...]) + vec_ref[OUT_BIAS : OUT_BIAS + 1]
@@ -240,37 +338,47 @@
     sums_ref[1:2] += col_sum(branch * branch)
 
 
-def mlp_kernel(
-    normed_ref,
-    cot_ref,
-    vec_ref,
-    fc_ref,
-    proj_ref,
-    mlp_ref,
-    back_ref,
-    dfc_ref,
-    dproj_ref,
-    bias_ref,
-    w_fc,
-    w_fc_t,
-    w_proj,
-    w_proj_t,
-    hidden,
-    grad_pre,
-):
-    tile = pl.program_id(0)
-    place(w_fc, fc_ref.at[0], 1, 2)
-    place(w_fc.at[pl.ds(D // 2, D // 2)], fc_ref.at[1], 1, 2)
-    place(w_proj.at[pl.ds(0, D // 2)], proj_ref.at[0], 1, 2)
-    place(w_proj.at[pl.ds(D // 2, D // 2)], proj_ref.at[1], 1, 2)
+def put_pieces(keep_ref, send_ref, grad, core, base):
+    height, width = keep_ref.shape[-2:]
+    for held, ref in enumerate((keep_ref, send_ref)):
+        for pair in range(ref.shape[0]):
+            piece = 2 * pair + (core ^ held)
+            for row in range(2):
+                top = pl.multiple_of(row * width + piece * height, 8)
+                for col in range(2):
+                    ref[pair, base + 2 * row + col] = grad[
+                        pl.ds(top, height), col * width : (col + 1) * width
+                    ].astype(BF)
+
+
+def mlp_kernel(place_ref, me_ref, normed_ref, cot_ref, vec_ref, *refs, first, paired):
+    fc_blocks, proj_blocks, refs = refs[:4], refs[4:8], refs[8:]
+    if first == 0:
+        before = None
+    else:
+        before, refs = refs[:2], refs[2:]
+    if paired:
+        mlp_ref, back_ref, keep_ref, send_ref, bias_ref = refs[:5]
+        refs = refs[5:]
+    else:
+        mlp_ref, back_ref, grad_ref, bias_ref = refs[:4]
+        refs = refs[4:]
+    w_fc, w_fc_t, w_proj, w_proj_t, hidden, grad_pre, whole_grad = refs
+    step = pl.program_id(0)
+    place(w_fc, fc_blocks, 2, 2)
+    place(w_proj, proj_blocks, 2, 2)
     w_fc_t[...] = w_fc[...].T
     w_proj_t[...] = w_proj[...].T
-    bias_row = vec_ref[pl.ds(FC_BIAS + tile, 1)]
-
-    @pl.when(tile == 0)
+    bias_row = vec_ref[pl.ds(FC_BIAS + first + step, 1)]
+
+    @pl.when(step == 0)
     def _():
-        mlp_ref[...] = jnp.zeros_like(mlp_ref)
-        back_ref[...] = jnp.zeros_like(back_ref)
+        if first == 0:
+            mlp_ref[...] = jnp.zeros_like(mlp_ref)
+            back_ref[...] = jnp.zeros_like(back_ref)
+        else:
+            mlp_ref[...] = before[0][...]
+            back_ref[...] = before[1][...]
 
     def chunk(index, total):
         rows = pl.ds(pl.multiple_of(index * TILE, TILE), TILE)
@@ -291,37 +399,40 @@
 
     count = normed_ref.shape[0]
     bias_ref[0] = lax.fori_loop(0, count // TILE, chunk, jnp.zeros((1, D), F32))
-    half = D // 2
-    dproj = tn(hidden[...], cot_ref[...]).astype(BF)
-    dfc = tn(normed_ref[...], grad_pre[...]).astype(BF)
-    for row in range(2):
-        for col in range(2):
-            part = (slice(row * half, (row + 1) * half), slice(col * half, (col + 1) * half))
-            dproj_ref[row, col] = dproj[part]
-            dfc_ref[row, col] = dfc[part]
+    for base, left, right in ((0, normed_ref, grad_pre), (4, hidden, cot_ref)):
+        if paired:
+            whole_grad[...] = tn(left[...], right[...])
+            put_pieces(keep_ref, send_ref, whole_grad, me_ref[0] % 2, base)
+        else:
+            pieces, _, _, height, width = grad_ref.shape
+            grad = tn(left[...], right[...]).astype(BF)
+            for row in range(2):
+                for col in range(2):
+                    for piece in range(pieces):
+                        top = row * width + piece * height
+                        grad_ref[piece, 0, base + 2 * row + col] = grad[
+                            top : top + height, col * width : (col + 1) * width
+                        ]
 
 
 def middle_kernel(
+    place_ref,
+    me_ref,
     middle_ref,
     mlp_ref,
     back_ref,
     cot_ref,
     att_ref,
     vec_ref,
-    blocks_ref,
-    output_ref,
-    grad_ref,
-    grad_att_ref,
-    dout_ref,
-    sums_ref,
-    weight,
-    branch,
+    *refs,
 ):
+    blocks, refs = refs[:4], refs[4:]
+    output_ref, grad_ref, grad_att_ref, keep_ref, send_ref, sums_ref, weight, branch, out_grad = refs
     step = pl.program_id(0)
 
     @pl.when(step == 0)
     def _():
-        place(weight, blocks_ref, 2, 2)
+        place(weight, blocks, 2, 2)
         sums_ref[...] = jnp.zeros_like(sums_ref)
 
     middle = middle_ref[...]
@@ -334,8 +445,8 @@
     grad = cot + norm_back(unit, root, vec_ref[LN2_GAIN : LN2_GAIN + 1], back)
     grad_ref[...] = grad
     low = grad.astype(BF)
+    branch[pl.ds(pl.multiple_of(step * TILE, TILE), TILE)] = low
     grad_att_ref[...] = nt(low, weight[...]).astype(BF)
-    branch[pl.ds(pl.multiple_of(step * TILE, TILE), TILE)] = low
     sums_ref[0:1] += col_sum(result * result)
     sums_ref[1:2] += col_sum(mlp * mlp)
     sums_ref[2:3] += col_sum(back * unit)
@@ -345,34 +456,35 @@
 
     @pl.when(step == pl.num_programs(0) - 1)
     def _():
-        half = D // 2
-        dout = tn(att_ref[...], branch[...]).astype(BF)
-        for row in range(2):
-            for col in range(2):
-                dout_ref[2 * row + col] = dout[
-                    row * half : (row + 1) * half, col * half : (col + 1) * half
-                ]
-
-
-def dqkv_kernel(normed_ref, dq_ref, dk_ref, dv_ref, grad_ref, sums_ref):
-    half = D // 2
-    sums_ref[0:1] = col_sum(dq_ref[...].astype(F32))
-    sums_ref[1:2] = col_sum(dv_ref[...].astype(F32))
+        out_grad[...] = tn(att_ref[...], branch[...])
+        put_pieces(keep_ref, send_ref, out_grad, me_ref[0] % 2, 0)
+
+
+def weight_back_kernel(
+    me_ref, normed_ref, dq_ref, dk_ref, dv_ref, keep_ref, send_ref, sums_ref, grad
+):
+    step = pl.program_id(0)
+
+    @pl.when(step == 0)
+    def _():
+        sums_ref[0:1] = col_sum(dq_ref[...].astype(F32))
+        sums_ref[1:2] = col_sum(dv_ref[...].astype(F32))
+
     for part, ref in enumerate((dq_ref, dk_ref, dv_ref)):
-        grad = tn(normed_ref[...], ref[...]).astype(BF)
-        for row in range(2):
-            for col in range(2):
-                grad_ref[row * 6 + part * 2 + col] = grad[
-                    row * half : (row + 1) * half, col * half : (col + 1) * half
-                ]
-
-
-def input_kernel(
-    x_ref, dq_ref, dk_ref, dv_ref, grad_ref, vec_ref, blocks_ref, out_ref, sums_ref, weight
-):
+
+        @pl.when(step == part)
+        def _():
+            grad[...] = tn(normed_ref[...], ref[...])
+
+    put_pieces(keep_ref, send_ref, grad, me_ref[0] % 2, 0)
+
+
+def input_kernel(place_ref, x_ref, dq_ref, dk_ref, dv_ref, grad_ref, vec_ref, *refs):
+    blocks, (out_ref, sums_ref, weight) = refs[:12], refs[12:]
+
     @pl.when(pl.program_id(0) == 0)
     def _():
-        place(weight, blocks_ref, 2, 6)
+        place(weight, blocks, 2, 6)
         sums_ref[...] = jnp.zeros_like(sums_ref)
 
     back = nt(dq_ref[...], weight[:, :D])
@@ -382,6 +494,18 @@
     out_ref[...] = grad_ref[...] + norm_back(unit, root, vec_ref[LN1_GAIN : LN1_GAIN + 1], back)
     sums_ref[0:1] += col_sum(back * unit)
     sums_ref[1:2] += col_sum(back)
+
+
+def lay_kernel(source_ref, *refs):
+    out_ref, pieces = refs[-2:]
+    begin = 0
+    for ref in refs[:-2]:
+        pieces[begin : begin + ref.shape[0]] = ref[...]
+        begin += ref.shape[0]
+    shards, own = out_ref.shape[:2]
+    for shard in range(shards):
+        for slot in range(own):
+            out_ref[shard, slot] = pieces[source_ref[shard * own + slot]]
 
 
 def factor_kernel(
@@ -396,13 +520,17 @@
     left_ref,
     right_new_ref,
     matrix_new_ref,
+    whole_grad,
     grad_t,
 ):
     rows = matrix_ref.shape[1]
-    grad = grad_ref[0]
+    pieces, _, height, _ = grad_ref.shape
+    for piece in range(pieces):
+        whole_grad[piece * height : (piece + 1) * height, :] = grad_ref[piece, 0]
+    grad = whole_grad[...]
     grad_t[...] = grad.T
     own = pl.ds(pl.multiple_of(shard_ref[0] * rows, rows), rows)
-    grad_rows = grad_ref[0, own, :]
+    grad_rows = whole_grad[own, :]
     rows_ref[0] = grad_rows.astype(F32)
     left_ref[0] = DECAY * left_stat_ref[0] + (1.0 - DECAY) * nn(grad_rows, grad_t[...])
     right_new_ref[0] = DECAY * right_stat_ref[0] + (1.0 - DECAY) * nn(grad_t[own, :], grad)
@@ -411,16 +539,60 @@
     matrix_new_ref[0] = matrix_ref[0] - MATRIX_RATE * update
 
 
-def whole(array):
-    return (array, array.shape, lambda *_: (0,) * array.ndim)
-
-
-def tokens_in(array, cols=None):
-    return (array, (TILE, cols or array.shape[1]), lambda i, *_: (i, 0))
-
-
-def out_whole(shape, dtype):
-    return (shape, dtype, shape, lambda *_: (0,) * len(shape))
+def core_sum_kernel(*refs):
+    out_ref = refs[-1]
+    begin = 0
+    for keep, sent in zip(refs[:-1:2], refs[1:-1:2]):
+        blocks = keep.shape[1]
+        out_ref[0, begin : begin + blocks] = (keep[0].astype(F32) + sent[0].astype(F32)).astype(BF)
+        begin += blocks
+
+
+def across_dp(values, bit):
+    count = lax.axis_size("dp")
+    return lax.ppermute(values, "dp", [(i, i ^ (1 << bit)) for i in range(count)])
+
+
+def across_fsdp(values, offset):
+    count = lax.axis_size("fsdp")
+    return lax.ppermute(values, "fsdp", [(i, i ^ offset) for i in range(count)])
+
+
+def core_sum(grads, name, ties=()):
+    ins = []
+    for keep, send in grads:
+        ins += [keep, across_dp(send, 0)]
+    pairs = ins[0].shape[0]
+    rest = ins[0].shape[2:]
+    blocks = sum(keep.shape[1] for keep, _ in grads)
+
+    def one(array):
+        return (array, (1,) + array.shape[1:], lambda i: (i, 0, 0, 0))
+
+    return call(
+        core_sum_kernel,
+        (pairs,),
+        [one(array) for array in ins],
+        [((pairs, blocks) + rest, BF, (1, blocks) + rest, lambda i: (i, 0, 0, 0))],
+        ties=ties,
+        name=name,
+    )[0]
+
+
+def plane_parts(values):
+    pairs = lax.axis_size("dp") // 2
+    groups = [[2 * pair + core for pair in range(pairs)] for core in range(2)]
+    return lax.all_to_all(values, "dp", 0, 0, axis_index_groups=groups, tiled=True)
+
+
+def everywhere_sum(values, bits):
+    for bit in range(bits):
+        values = values + across_dp(values, bit)
+    offset = 1
+    while offset < lax.axis_size("fsdp"):
+        values = values + across_fsdp(values, offset)
+        offset *= 2
+    return values
 
 
 def per_device(
@@ -438,12 +610,18 @@
 ):
     dp_count = lax.axis_size("dp")
     fsdp_count = lax.axis_size("fsdp")
+    bits = dp_count.bit_length() - 1
     own_blocks, own_rows, width = matrices.shape
     blocks = own_blocks * dp_count
+    height = width // dp_count
+    me = lax.axis_index("dp").astype(jnp.int32).reshape(1)
+    shard = lax.axis_index("fsdp").astype(jnp.int32).reshape(1)
+    half = lax.axis_index("fsdp")
+    half = sum((half >> bit) & 1 for bit in range(fsdp_count.bit_length())) % 2
+    half = half.astype(jnp.int32).reshape(1)
     slot_place = block_slot % own_blocks * dp_count + block_slot // own_blocks
-    low_shards = matrices.astype(BF)
-    gathered = lax.all_gather(low_shards, ("dp", "fsdp"), axis=1, tiled=True)
-    used = jnp.take(gathered.reshape(blocks, width, width), slot_place, axis=0)
+    gathered = lax.all_gather(matrices.astype(BF), ("dp", "fsdp"), axis=1, tiled=True)
+    gathered = gathered.reshape(blocks, width, width)
     right_whole = lax.all_gather(right_root.astype(BF), "fsdp", axis=1, tiled=True)
 
     vec = vectors.reshape(-1, D)
@@ -451,21 +629,23 @@
     rows_here, docs = doc_lengths.shape
     seq_len = count // rows_here
     steps = count // TILE
-    weight_scratch = [pltpu.VMEM((D, 3 * D), BF)]
-    small_scratch = [pltpu.VMEM((D, D), BF)]
-    qkv_in = (used, (12, width, width), lambda *_: (0, 0, 0))
-    out_in = (used, (4, width, width), lambda *_: (3, 0, 0))
+
+    def block_of(number):
+        return (gathered, (1, width, width), lambda t, at, *_: (at[number(t)], 0, 0))
+
+    qkv_in = [block_of(lambda t, u=u: u) for u in range(12)]
+    out_in = [block_of(lambda t, u=u: 12 + u) for u in range(4)]
 
     normed1, projected = call(
         qkv_kernel,
         (steps,),
-        [tokens_in(tokens), whole(vec), qkv_in],
+        [tokens_in(tokens), whole(vec)] + qkv_in,
         [
-            ((count, D), BF, (TILE, D), lambda i: (i, 0)),
-            ((count, 3 * D), BF, (TILE, 3 * D), lambda i: (i, 0)),
+            ((count, D), BF, (TILE, D), lambda i, *_: (i, 0)),
+            ((count, 3 * D), BF, (TILE, 3 * D), lambda i, *_: (i, 0)),
         ],
-        weight_scratch,
-        flops=2 * count * D * 3 * D,
+        [pltpu.VMEM((D, 3 * D), BF)],
+        scalars=[slot_place],
         name="qkv",
     )
 
@@ -487,7 +667,6 @@
             ],
             [pltpu.VMEM((bias_rows, TILE), F32), pltpu.VMEM((PAIR, seq_len), F32)],
             scalars=[doc_lengths],
-            flops=8 * seq_len * seq_len * D,
             name="attend",
         )
         attended.append(one)
@@ -497,43 +676,76 @@
     middle, normed2, sums_mid = call(
         out_kernel,
         (steps,),
-        [tokens_in(attended), tokens_in(tokens), whole(vec), out_in],
+        [tokens_in(attended), tokens_in(tokens), whole(vec)] + out_in,
         [
-            ((count, D), F32, (TILE, D), lambda i: (i, 0)),
-            ((count, D), BF, (TILE, D), lambda i: (i, 0)),
+            ((count, D), F32, (TILE, D), lambda i, *_: (i, 0)),
+            ((count, D), BF, (TILE, D), lambda i, *_: (i, 0)),
             out_whole((8, D), F32),
         ],
-        small_scratch,
-        flops=2 * count * D * D,
+        [pltpu.VMEM((D, D), BF)],
+        scalars=[slot_place],
         name="attn_out",
     )
 
-    ff_tiles = FF // D
-    fc_view = used.reshape(6, 8, width, width)
-    proj_view = used.reshape(24, 2, width, width)
-    mlp, back2, dfc, dproj, fc_bias_grad = call(
-        mlp_kernel,
-        (ff_tiles,),
-        [
-            whole(normed2),
-            whole(cotangent),
-            whole(vec),
-            (fc_view, (2, 2, width, width), lambda t: (1, t, 0, 0)),
-            (proj_view, (2, 2, width, width), lambda t: (8 + t, 0, 0, 0)),
-        ],
-        [
-            out_whole((count, D), F32),
-            out_whole((count, D), F32),
-            ((2, 8, width, width), BF, (2, 2, width, width), lambda t: (0, t, 0, 0)),
-            ((8, 2, width, width), BF, (2, 2, width, width), lambda t: (t, 0, 0, 0)),
-            ((ff_tiles, 1, D), F32, (1, 1, D), lambda t: (t, 0, 0)),
-        ],
-        [pltpu.VMEM((D, D), BF)] * 4 + [pltpu.VMEM((count, D), BF)] * 2,
-        flops=12 * count * D * FF,
-        name="mlp",
-    )
-
-    output, grad_middle, grad_attended, dout, sums_back = call(
+    ff_cols = FF // width
+    pair_count = dp_count // 2
+    tile_parts = ((0, FIRST_TILES), (FIRST_TILES, FF // D))
+    held, fc_sums, mlp_grads = [], [], []
+    for start, stop in tile_parts:
+        tiles = stop - start
+        fc_in = [
+            block_of(lambda t, r=r, c=c, s=start: 16 + r * ff_cols + 2 * (t + s) + c)
+            for r in range(2)
+            for c in range(2)
+        ]
+        proj_in = [
+            block_of(lambda t, r=r, c=c, s=start: 16 + 2 * ff_cols + 2 * (2 * (t + s) + r) + c)
+            for r in range(2)
+            for c in range(2)
+        ]
+        if start == 0:
+            pieces = [
+                (
+                    (dp_count, tiles, 8, height, width),
+                    BF,
+                    (dp_count, 1, 8, height, width),
+                    lambda t, *_: (0, t, 0, 0, 0),
+                )
+            ]
+        else:
+            pieces = [
+                (
+                    (pair_count, tiles * 8, height, width),
+                    BF,
+                    (pair_count, 8, height, width),
+                    lambda t, *_: (0, t, 0, 0),
+                )
+            ] * 2
+        mlp, back2, *grads, fc_sum = call(
+            functools.partial(mlp_kernel, first=start, paired=start > 0),
+            (tiles,),
+            [whole(normed2), whole(cotangent), whole(vec)]
+            + fc_in
+            + proj_in
+            + [whole(array) for array in held],
+            [out_whole((count, D), F32), out_whole((count, D), F32)]
+            + pieces
+            + [((tiles, 1, D), F32, (1, 1, D), lambda t, *_: (t, 0, 0))],
+            [pltpu.VMEM((D, D), BF)] * 4
+            + [pltpu.VMEM((count, D), BF)] * 2
+            + [pltpu.VMEM((D, D), F32)],
+            scalars=[slot_place, me],
+            ties=[right_whole] if start else [],
+            name="mlp",
+        )
+        held = [mlp, back2]
+        fc_sums.append(fc_sum)
+        mlp_grads.append(grads)
+    first_grads = lax.psum_scatter(
+        mlp_grads[0][0].reshape(-1, width), "dp", scatter_dimension=0, tiled=True
+    )
+
+    output, grad_middle, grad_attended, *out_grads, sums_back = call(
         middle_kernel,
         (steps,),
         [
@@ -543,20 +755,25 @@
             tokens_in(cotangent),
             whole(attended),
             whole(vec),
-            out_in,
-        ],
+        ]
+        + out_in,
         [
-            ((count, D), BF, (TILE, D), lambda i: (i, 0)),
-            ((count, D), F32, (TILE, D), lambda i: (i, 0)),
-            ((count, D), BF, (TILE, D), lambda i: (i, 0)),
-            out_whole((4, width, width), BF),
+            ((count, D), BF, (TILE, D), lambda i, *_: (i, 0)),
+            ((count, D), F32, (TILE, D), lambda i, *_: (i, 0)),
+            ((count, D), BF, (TILE, D), lambda i, *_: (i, 0)),
+            out_whole((pair_count, 4, height, width), BF),
+            out_whole((pair_count, 4, height, width), BF),
             out_whole((8, D), F32),
         ],
-        small_scratch + [pltpu.VMEM((count, D), BF)],
-        flops=4 * count * D * D,
+        [pltpu.VMEM((D, D), BF), pltpu.VMEM((count, D), BF), pltpu.VMEM((D, D), F32)],
+        scalars=[slot_place, me],
         name="middle_back",
     )
 
+    second_core = core_sum([mlp_grads[1], out_grads], "second_core")
+    first_halves = plane_sum(first_grads.reshape(1, -1, height, width), half, [], "first_split")
+    first_half = line_half(first_halves, [grad_attended], "first_half")
+    second_parts = plane_parts(second_core)
     query_grads, key_grads, value_grads = [], [], []
     for row in range(rows_here):
         grads = call(
@@ -576,24 +793,33 @@
                 pltpu.VMEM((PAIR, seq_len), F32),
             ],
             scalars=[doc_lengths],
-            flops=20 * seq_len * seq_len * D,
+            ties=[second_core, first_halves[0]],
             name="attend_back",
         )
-        for held, one in zip((query_grads, key_grads, value_grads), grads):
-            held.append(one)
+        for kept, one in zip((query_grads, key_grads, value_grads), grads):
+            kept.append(one)
     dq, dk, dv = [
-        held[0] if rows_here == 1 else jnp.concatenate(held, axis=0)
-        for held in (query_grads, key_grads, value_grads)
+        kept[0] if rows_here == 1 else jnp.concatenate(kept, axis=0)
+        for kept in (query_grads, key_grads, value_grads)
     ]
 
-    dqkv, sums_qkv = call(
-        dqkv_kernel,
-        (1,),
-        [whole(normed1), whole(dq), whole(dk), whole(dv)],
-        [out_whole((12, width, width), BF), out_whole((8, D), F32)],
-        flops=2 * count * D * 3 * D,
+    half_shape = (pair_count, 12, height, width)
+    keep, send, sums_qkv = call(
+        weight_back_kernel,
+        (3,),
+        [whole(array) for array in (normed1, dq, dk, dv)],
+        [(half_shape, BF, (pair_count, 4, height, width), lambda p, *_: (0, p, 0, 0))] * 2
+        + [out_whole((8, D), F32)],
+        [pltpu.VMEM((D, D), F32)],
+        scalars=[me],
+        ties=[first_half],
         name="qkv_weight_back",
     )
+    first_total = line_rest(first_half, [keep], "first_rest")
+    third_core = core_sum([(keep, send)], "third_core")
+    second_halves = plane_sum(second_parts, half, [], "second_plane")
+    third_parts = plane_parts(third_core)
+
     x_grad, sums_in = call(
         input_kernel,
         (steps,),
@@ -604,42 +830,61 @@
             tokens_in(dv),
             tokens_in(grad_middle),
             whole(vec),
-            qkv_in,
-        ],
-        [((count, D), F32, (TILE, D), lambda i: (i, 0)), out_whole((8, D), F32)],
-        weight_scratch,
-        flops=2 * count * D * 3 * D,
+        ]
+        + qkv_in,
+        [((count, D), F32, (TILE, D), lambda i, *_: (i, 0)), out_whole((8, D), F32)],
+        [pltpu.VMEM((D, 3 * D), BF)],
+        scalars=[slot_place],
+        ties=[second_halves[0], third_core, first_total],
         name="input_back",
     )
 
-    vector_local = jnp.concatenate(
-        [
-            sums_in[0],
-            sums_in[1],
-            sums_qkv[0],
-            sums_qkv[1],
-            sums_back[4],
-            sums_back[2],
-            sums_back[3],
-            sums_back[5],
-            fc_bias_grad.reshape(-1),
-        ]
-    )
-    square_terms = jnp.stack(
-        [jnp.sum(sums_mid[0]), jnp.sum(sums_back[0]), jnp.sum(sums_mid[1]), jnp.sum(sums_back[1])]
-    )
-    vector_grad, square_sums = lax.psum((vector_local, square_terms), ("dp", "fsdp"))
-
-    grads_used = jnp.concatenate(
-        [dqkv, dout, dfc.reshape(16, width, width), dproj.reshape(16, width, width)], axis=0
-    )
-    grads_laid = jnp.take(grads_used, jnp.argsort(slot_place), axis=0).reshape(
-        own_blocks, dp_count * width, width
-    )
-    grad_rows = lax.psum_scatter(grads_laid, ("dp", "fsdp"), scatter_dimension=1, tiled=True)
-    grad_whole = lax.all_gather(grad_rows, "fsdp", axis=1, tiled=True)
-
-    shard = lax.axis_index("fsdp").astype(jnp.int32).reshape(1)
+    second_half = line_half(second_halves, [x_grad], "second_half")
+    second_total = line_rest(second_half, [], "second_rest")
+    vector_local = call(
+        pack_kernel,
+        (1,),
+        [whole(array) for array in (sums_in, sums_qkv, sums_back, sums_mid, *fc_sums)],
+        [out_whole((16, D), F32)],
+        name="pack",
+    )[0]
+    vector_sums = everywhere_sum(vector_local, bits)
+    third_halves = plane_sum(third_parts, half, [second_half], "third_plane")
+    third_total = line_rest(line_half(third_halves, [], "third_half"), [], "third_rest")
+    vector_grad = vector_sums[:12].reshape(-1)
+    square_sums = vector_sums[12, :4]
+
+    order = []
+    for tile in range(FF // D):
+        order += [16 + r * ff_cols + 2 * tile + c for r in range(2) for c in range(2)]
+        order += [16 + 2 * ff_cols + 2 * (2 * tile + r) + c for r in range(2) for c in range(2)]
+    order += list(range(12, 16))
+    order += [r * 6 + 2 * part + c for part in range(3) for r in range(2) for c in range(2)]
+    numbers = jnp.arange(blocks, dtype=jnp.int32)
+    standing = jnp.array([order.index(u) for u in range(blocks)], jnp.int32)
+    source = jnp.sum(
+        jnp.where(block_slot[None, :] == numbers[:, None], standing[None, :], 0), axis=1
+    )
+    begin = 0
+    spread = []
+    for total in (first_total, second_total, third_total):
+        size = total.shape[0]
+        inside = source - begin
+        moved = begin + (inside // size ^ half[0]) * size + inside % size
+        source = jnp.where((inside >= 0) & (inside < size * 2), moved, source)
+        begin += size * 2
+        spread += line_spread(total)
+    laid = call(
+        lay_kernel,
+        (1,),
+        [whole(array) for array in spread],
+        [out_whole((dp_count, own_blocks, height, width), BF)],
+        [pltpu.VMEM((blocks, height, width), BF)],
+        scalars=[source],
+        ties=[vector_sums],
+        name="lay",
+    )[0]
+    grad_whole = lax.all_to_all(laid, "dp", 0, 0, tiled=True)
 
     def block_in(array):
         return (array, (1,) + array.shape[1:], lambda b, *_: (b, 0, 0))
@@ -647,14 +892,11 @@
     matrix_grad, left_new, right_new, matrix_new = call(
         factor_kernel,
         (own_blocks,),
-        [
-            block_in(a)
-            for a in (grad_whole, right_whole, matrices, left_stat, right_stat, left_root)
-        ],
+        [(grad_whole, (dp_count, 1, height, width), lambda b, *_: (0, b, 0, 0))]
+        + [block_in(a) for a in (right_whole, matrices, left_stat, right_stat, left_root)],
         [(matrices.shape, F32, (1, own_rows, width), lambda b, *_: (b, 0, 0))] * 4,
-        [pltpu.VMEM((width, width), BF)],
+        [pltpu.VMEM((width, width), BF)] * 2,
         scalars=[shard],
-        flops=8 * own_blocks * own_rows * width * width,
         name="factor",
     )
 

time: 545 us -> 430 us (0.79)
  waiting for transfers between devices: 265 us -> 180 us
  Pallas kernels: 143 us -> 190 us
  other arithmetic: 50.6 us -> 6.67 us
  blocking collectives: 40.4 us -> 0 us
  starting transfers between devices: 0.17 us -> 28.6 us
  local copies, waits for them, and re-layouts: 28.9 us -> 10 us
    reduce_scatter x1, waiting for transfers between devices: 161 us -> 0.02 us  [per_device(): lax.psum_scatter(mlp_grads[0][0].reshape(-1, width), 'dp', scatter_dimens...]
    ppermute x0 -> x17, waiting for transfers between devices: none -> 51.5 us  [the longest x11 43.1 us: across_fsdp(): return lax.ppermute(values, 'fsdp', [(i, i ^ offset) for i in range(count)])]
    pallas_call x9 -> x23, Pallas kernels: 143 us -> 190 us  [call(): pl.pallas_call(body, grid_spec=spec, out_shape=[jax.ShapeDtypeStruct(shap...]
    psum x1 -> x0, blocking collectives: 40.4 us -> none  [per_device(): lax.psum((vector_local, square_terms), ('dp', 'fsdp'))]
    select_n x4 -> x1, other arithmetic: 26.4 us -> 0.56 us  [per_device(): source = jnp.where((inside >= 0) & (inside < size * 2), moved, source)]
    gather x2 -> x0, local copies, waits for them, and re-layouts: 24.7 us -> none  [the longest x1 12.4 us: per_device(): used = jnp.take(gathered.reshape(blocks, width, width), slot_place, axis=0)]
    all_to_all x0 -> x3, waiting for transfers between devices: none -> 21.9 us  [the longest x1 21.8 us: per_device(): grad_whole = lax.all_to_all(laid, 'dp', 0, 0, tiled=True)]
    ppermute x0 -> x17, starting transfers between devices: none -> 16.2 us  [the longest x11 12.1 us: across_fsdp(): return lax.ppermute(values, 'fsdp', [(i, i ^ offset) for i in range(count)])]
  transfers between devices with their start and end apart: 4 -> 23, of which waited for: 2 -> 10; matrix products, arithmetic and copies ran while one was open for 2% -> 1% of each run, Pallas kernels for 2% -> 42%
where the time goes in v2:
time: 430 us; the launch traced here: 429 us
  Pallas kernels  190 us (44%)
  waiting for transfers between devices  180 us (42%)
  starting transfers between devices  28.6 us (7%)
  between operations  14 us (3%)
  local copies, waits for them, and re-layouts  10 us (2%)
  other arithmetic  6.67 us (2%)
    pallas_call x23, Pallas kernels, call(): pl.pallas_call(body, grid_spec=spec, out_shape=[jax.ShapeDtypeStruct(shap...  190 us
    all_gather x1, waiting for transfers between devices, per_device(): lax.all_gather(matrices.astype(BF), ('dp', 'fsdp'), axis=1, tiled=True)  106 us
    ppermute x11, waiting for transfers between devices, across_fsdp(): return lax.ppermute(values, 'fsdp', [(i, i ^ offset) for i in range(count)])  43.1 us
    all_to_all x1, waiting for transfers between devices, per_device(): grad_whole = lax.all_to_all(laid, 'dp', 0, 0, tiled=True)  21.8 us
    ppermute x11, starting transfers between devices, across_fsdp(): return lax.ppermute(values, 'fsdp', [(i, i ^ offset) for i in range(count)])  12.1 us
    unnamed x48, local copies, waits for them, and re-layouts  9.38 us
  transfers between devices with their start and end apart: 23, of which 10 were waited for; matrix products, arithmetic and copies ran while one was open for 1% of the time, Pallas kernels for 42%

profile of v2, /device:TPU:0, one launch (start us, length us, event | category | flops | bytes accessed | tf_op | source)
XLA Modules:
  0.0 428.5 jit_solution(12782879930614724250)
XLA Ops:
  7.3 2.0 convert_element_type.6
  9.4 0.8 convert_element_type.7
  11.4 106.2 %all-gather.3.cloned.1.call-done = bf16[6,3072,384]{2,1,0:T(8,128)(2,1)} async-done(((bf16[6,96,384]{2,1,0:T(8,128)(2,1)}), bf16[6,3072,384]{2,1,0:T(8,128)(2,1)}) %all-gather.3.cloned.1.call-update) | async-done | bytes 14155792 | tf_op jit(solution)/shard_map/all_gather | solution.py:623
  117.7 9.7 %qkv.1 = (bf16[1024,768]{1,0:T(8,128)(2,1)}, bf16[1024,2304]{1,0:T(8,128)(2,1)}) custom-call(s32[48]{0:T(128)} %fusion.5.refs_0_, bf16[1024,768]{1,0:T(8,128)(2,1)} %refs_1_.3, f32[12,768]{1,0:T(8,128)} %reshape.50.refs_2_.refs_3_.refs_4_.refs_7_.refs_6_, bf16[48,384,384]{2,1,0:T(8,128)(2,1)} %bitcast.9, bf16[48,384,384]{2,1,0:T(8,128)(2,1)} %bitcast.10, ...), custom_call_target="tpu_custom_call" | custom-call | flops 1024 | bytes 1024 | tf_op jit(solution)/shard_map/qkv/pallas_call | solution.py:88
  127.4 24.3 %attend.1 = (bf16[1024,768]{1,0:T(8,128)(2,1)}, f32[6,2,1024]{2,1,0:T(2,128)}) custom-call(s32[1,8]{1,0:T(1,128)} %refs_0_.3, bf16[1024,2304]{1,0:T(8,128)(2,1)} %get-tuple-element.50.refs_1_.refs_2_.refs_3_, bf16[1024,2304]{1,0:T(8,128)(2,1)} %get-tuple-element.50.refs_1_.refs_2_.refs_3_, bf16[1024,2304]{1,0:T(8,128)(2,1)} %get-tuple-element.50.refs_1_.refs_2_.refs_3_), custom_call_target="tpu_custom_call" | custom-call | flops 1024 | bytes 1024 | tf_op jit(solution)/shard_map/attend/pallas_call | solution.py:88
  151.7 6.8 %attn_out.1 = (f32[1024,768]{1,0:T(8,128)}, bf16[1024,768]{1,0:T(8,128)(2,1)}, f32[8,768]{1,0:T(8,128)}) custom-call(s32[48]{0:T(128)} %fusion.5.refs_0_, bf16[1024,768]{1,0:T(8,128)(2,1)} %get-tuple-element.51.refs_1_.refs_6_.refs_4_, bf16[1024,768]{1,0:T(8,128)(2,1)} %refs_1_.3, f32[12,768]{1,0:T(8,128)} %reshape.50.refs_2_.refs_3_.refs_4_.refs_7_.refs_6_, ...), custom_call_target="tpu_custom_call" | custom-call | flops 1024 | bytes 1024 | tf_op jit(solution)/shard_map/attn_out/pallas_call | solution.py:88
  158.5 24.3 %mlp.2 = (f32[1024,768]{1,0:T(8,128)}, f32[1024,768]{1,0:T(8,128)}, bf16[8,2,8,48,384]{4,3,2,1,0:T(8,128)(2,1)}, f32[2,1,768]{2,1,0:T(1,128)}) custom-call(s32[48]{0:T(128)} %fusion.5.refs_0_, s32[1]{0:T(128)} %bitcast.refs_1_.refs_0_, bf16[1024,768]{1,0:T(8,128)(2,1)} %get-tuple-element.53.refs_2_, bf16[1024,768]{1,0:T(8,128)(2,1)} %refs_5_.2, ...), custom_call_target="tpu_custom_call" | custom-call | flops 1024 | bytes 1024 | tf_op jit(solution)/shard_map/mlp/pallas_call | solution.py:88
  182.8 29.7 %mlp.3 = (f32[1024,768]{1,0:T(8,128)}, f32[1024,768]{1,0:T(8,128)}, bf16[4,16,48,384]{3,2,1,0:T(8,128)(2,1)}, bf16[4,16,48,384]{3,2,1,0:T(8,128)(2,1)}, f32[2,1,768]{2,1,0:T(1,128)}) custom-call(s32[48]{0:T(128)} %fusion.5.refs_0_, s32[1]{0:T(128)} %bitcast.refs_1_.refs_0_, bf16[1024,768]{1,0:T(8,128)(2,1)} %get-tuple-element.53.refs_2_, ...), custom_call_target="tpu_custom_call" | custom-call | flops 1024 | bytes 1024 | tf_op jit(solution)/shard_map/mlp/pallas_call | solution.py:88
  212.9 13.0 %middle_back.1 = (bf16[1024,768]{1,0:T(8,128)(2,1)}, f32[1024,768]{1,0:T(8,128)}, bf16[1024,768]{1,0:T(8,128)(2,1)}, bf16[4,4,48,384]{3,2,1,0:T(8,128)(2,1)}, bf...) custom-call(s32[48]{0:T(128)} %fusion.5.refs_0_, s32[1]{0:T(128)} %bitcast.refs_1_.refs_0_, ...), custom_call_target="tpu_custom_call" | custom-call | flops 1024 | bytes 1024 | tf_op jit(solution)/shard_map/middle_back/pallas_call | solution.py:88
  226.2 2.0 collective-permute-done.1.refs_3_
  228.2 0.8 copy-done.6
  229.8 4.9 %second_core.1.refs_7_ = bf16[4,20,48,384]{3,2,1,0:T(8,128)(2,1)} custom-call(bf16[4,16,48,384]{3,2,1,0:T(8,128)(2,1)} %get-tuple-element.61.refs_0_, bf16[4,16,48,384]{3,2,1,0:T(8,128)(2,1)} %copy-done.4, bf16[4,4,48,384]{3,2,1,0:T(8,128)(2,1)} %get-tuple-element.63.refs_2_, bf16[4,4,48,384]{3,2,1,0:T(8,128)(2,1)} %copy-done.6), custom_call_target="tpu_custom_call" | custom-call | flops 1024 | bytes 1024 | tf_op jit(solution)/shard_map/second_core/pallas_call | solution.py:88
  234.7 3.9 all-to-all-start
  238.6 1.9 first_split.1
  241.1 22.6 %attend_back.1 = (bf16[1024,768]{1,0:T(8,128)(2,1)}, bf16[1024,768]{1,0:T(8,128)(2,1)}, bf16[1024,768]{1,0:T(8,128)(2,1)}) custom-call(s32[1,8]{1,0:T(1,128)} %refs_0_.3, bf16[1024,2304]{1,0:T(8,128)(2,1)} %get-tuple-element.50.refs_1_.refs_2_.refs_3_, bf16[1024,2304]{1,0:T(8,128)(2,1)} %get-tuple-element.50.refs_1_.refs_2_.refs_3_, ...), custom_call_target="tpu_custom_call" | custom-call | flops 1024 | bytes 1024 | tf_op jit(solution)/shard_map/attend_back/pallas_call | solution.py:88
  264.5 1.8 first_half.1.refs_5_.refs_0_
  266.3 8.7 %qkv_weight_back.1 = (bf16[4,12,48,384]{3,2,1,0:T(8,128)(2,1)}, bf16[4,12,48,384]{3,2,1,0:T(8,128)(2,1)}, f32[8,768]{1,0:T(8,128)}) custom-call(s32[1]{0:T(128)} %bitcast.refs_1_.refs_0_, bf16[1024,768]{1,0:T(8,128)(2,1)} %get-tuple-element.72.refs_1_, bf16[1024,768]{1,0:T(8,128)(2,1)} %get-tuple-element.67.refs_2_, ...), custom_call_target="tpu_custom_call" | custom-call | flops 1024 | bytes 1024 | tf_op jit(solution)/shard_map/qkv_weight_back/pallas_call | solution.py:88
  275.0 4.0 collective-permute-done.3.refs_1_
  279.0 4.1 third_core.1.refs_20_
  283.1 1.6 copy-done
  284.7 4.7 %all-to-all-start.1 = ((bf16[4,12,48,384]{3,2,1,0:T(8,128)(2,1)}), bf16[4,12,48,384]{3,2,1,0:T(8,128)(2,1)}, u32[]{:S(2)}, u32[]{:S(2)}) async-start(bf16[4,12,48,384]{3,2,1,0:T(8,128)(2,1)} %third_core.1.refs_20_), calls=%async_computation.2 | async-start | bytes 3538944 | tf_op jit(solution)/shard_map/all_to_all | solution.py:585
  289.4 3.0 second_plane.1
  292.4 1.5 collective-permute-start.6
  293.9 1.0 collective-permute-start.4
  294.8 15.2 %collective-permute-done.4.refs_1_ = bf16[8,48,384]{2,1,0:T(8,128)(2,1)S(1)} collective-permute-done((bf16[8,48,384]{2,1,0:T(8,128)(2,1)S(1)}, bf16[8,48,384]{2,1,0:T(8,128)(2,1)S(1)}, u32[]{:S(2)}, u32[]{:S(2)}) %collective-permute-start.4) | collective-permute-done | bytes 294944 | tf_op jit(solution)/shard_map/ppermute | solution.py:558
  310.8 1.8 first_rest.1.refs_21_.refs_1_
  312.6 11.0 %input_back.1 = (f32[1024,768]{1,0:T(8,128)}, f32[8,768]{1,0:T(8,128)}) custom-call(s32[48]{0:T(128)} %fusion.5.refs_0_, bf16[1024,768]{1,0:T(8,128)(2,1)} %refs_1_.3, bf16[1024,768]{1,0:T(8,128)(2,1)} %get-tuple-element.67.refs_2_, bf16[1024,768]{1,0:T(8,128)(2,1)} %get-tuple-element.68.refs_3_, bf16[1024,768]{1,0:T(8,128)(2,1)} %get-tuple-element.69.refs_4_, ...), custom_call_target="tpu_custom_call" | custom-call | flops 1024 | bytes 1024 | tf_op jit(solution)/shard_map/input_back/pallas_call | solution.py:88
  324.4 1.9 second_half.1.refs_0_.refs_3_
  326.3 2.7 collective-permute-start.7
  329.1 2.3 third_plane.1
  331.5 1.6 pack.1
  333.1 9.9 %collective-permute-done.9.refs_1_ = bf16[6,48,384]{2,1,0:T(8,128)(2,1)S(1)} collective-permute-done((bf16[6,48,384]{2,1,0:T(8,128)(2,1)}, bf16[6,48,384]{2,1,0:T(8,128)(2,1)S(1)}, u32[]{:S(2)}, u32[]{:S(2)}) %collective-permute-start.9) | collective-permute-done | bytes 221216 | tf_op jit(solution)/shard_map/ppermute | solution.py:558
  343.7 1.8 third_half.1.refs_0_
  345.5 2.6 collective-permute-start.10
  348.9 1.7 collective-permute-start.13
  350.6 2.4 collective-permute-done.13
  353.0 1.8 collective-permute-start.14
  355.5 1.9 second_rest.1.refs_3_
  357.4 2.0 collective-permute-start.5
  359.7 14.4 %collective-permute-done.15 = f32[16,768]{1,0:T(8,128)S(1)} collective-permute-done((f32[16,768]{1,0:T(8,128)S(1)}, f32[16,768]{1,0:T(8,128)S(1)}, u32[]{:S(2)}, u32[]{:S(2)}) %collective-permute-start.15) | collective-permute-done | bytes 49184 | tf_op jit(solution)/shard_map/ppermute | solution.py:558
  374.9 1.8 third_rest.1.refs_5_
  376.6 1.5 collective-permute-start.11
  380.1 2.6 collective-permute-done.11.refs_6_
  383.5 3.6 lay.1
  387.1 3.7 all-to-all-start.2
  392.0 21.8 %all-to-all-done.2.refs_1_ = bf16[8,6,48,384]{3,2,1,0:T(8,128)(2,1)S(1)} async-done(((bf16[8,6,48,384]{3,2,1,0:T(8,128)(2,1)}), bf16[8,6,48,384]{3,2,1,0:T(8,128)(2,1)S(1)}, u32[]{:S(2)}, u32[]{:S(2)}) %all-to-all-start.2) | async-done | bytes 1769504 | tf_op jit(solution)/shard_map/all_to_all | solution.py:887
  413.9 1.2 copy-done.1
  415.1 6.9 %factor.1 = (f32[6,96,384]{2,1,0:T(8,128)}, f32[6,96,384]{2,1,0:T(8,128)}, f32[6,96,384]{2,1,0:T(8,128)}, f32[6,96,384]{2,1,0:T(8,128)}) custom-call(s32[1]{0:T(128)} %bitcast.5.refs_0_, bf16[8,6,48,384]{3,2,1,0:T(8,128)(2,1)} %copy-done.1, bf16[6,384,384]{2,1,0:T(8,128)(2,1)} %all-gather.5.cloned.1.call-done.refs_15_.refs_2_, f32[6,96,384]{2,1,0:T(8,128)} %refs_3_.5, ...), custom_call_target="tpu_custom_call" | custom-call | flops 1024 | bytes 1024 | tf_op jit(solution)/shard_map/factor/pallas_call | solution.py:88
  (86 shorter events, 12.7 us)
Async XLA Ops:
  7.2 2.2 copy-start.5
  7.2 3.1 copy-start.17
  7.2 3.7 copy-start.21
  7.2 110.5 %all-gather.3.cloned.1.call-start = ((), (), s32[]{:S(2)}) async-start(), calls=%async_computation.4 | async-start | bytes 14598144 | tf_op jit(solution)/shard_map/all_gather | solution.py:623
  9.3 173.5 %all-gather.5.cloned.1.call-start = ((), (), s32[]{:S(2)}) async-start(), calls=%async_computation.5 | async-start | bytes 2211840 | tf_op jit(solution)/shard_map/all_gather | solution.py:625
  10.2 228.4 %reduce-scatter.2.cloned.1.call-start = ((), (), s32[]{:S(2)}) async-start(), calls=%async_computation.6 | async-start | bytes 5308416 | tf_op jit(solution)/shard_map/reduce_scatter | solution.py:744
  212.5 15.7 %collective-permute-start = (bf16[4,16,48,384]{3,2,1,0:T(8,128)(2,1)}, bf16[4,16,48,384]{3,2,1,0:T(8,128)(2,1)S(1)}, u32[]{:S(2)}, u32[]{:S(2)}) collective-permute-start(bf16[4,16,48,384]{3,2,1,0:T(8,128)(2,1)} %get-tuple-element.62), channel_id=1, source_target_pairs={{0,4},{4,0},{8,12},{12,8},{16,20},{20,16},{24,28},{28,24},{1,5},{5... | collective-permute-start | bytes 7077896 | tf_op jit(solution)/shard_map/ppermute | solution.py:553
  225.9 2.3 collective-permute-start.1
  228.2 0.8 copy-start.6
  228.2 1.6 copy-start.4
  234.7 48.4 %all-to-all-start = ((bf16[4,20,48,384]{3,2,1,0:T(8,128)(2,1)}), bf16[4,20,48,384]{3,2,1,0:T(8,128)(2,1)S(1)}, u32[]{:S(2)}, u32[]{:S(2)}) async-start(bf16[4,20,48,384]{3,2,1,0:T(8,128)(2,1)} %second_core.1.refs_7_), calls=%async_computation.1 | async-start | bytes 5898240 | tf_op jit(solution)/shard_map/all_to_all | solution.py:585
  240.6 23.2 %collective-permute-start.2 = (bf16[8,48,384]{2,1,0:T(8,128)(2,1)}, bf16[8,48,384]{2,1,0:T(8,128)(2,1)S(1)}, u32[]{:S(2)}, u32[]{:S(2)}) collective-permute-start(bf16[8,48,384]{2,1,0:T(8,128)(2,1)} %get-tuple-element.73), channel_id=1, source_target_pairs={{0,1},{1,0},{2,3},{3,2},{4,5},{5,4},{6,7},{7,6},{8,9},{9,8},{10,11... | collective-permute-start | bytes 884744 | tf_op jit(solution)/shard_map/ppermute | solution.py:558
  263.7 0.7 copy-start.11
  275.0 4.0 collective-permute-start.3
  283.1 1.6 copy-start
  284.7 44.3 %all-to-all-start.1 = ((bf16[4,12,48,384]{3,2,1,0:T(8,128)(2,1)}), bf16[4,12,48,384]{3,2,1,0:T(8,128)(2,1)}, u32[]{:S(2)}, u32[]{:S(2)}) async-start(bf16[4,12,48,384]{3,2,1,0:T(8,128)(2,1)} %third_core.1.refs_20_), calls=%async_computation.2 | async-start | bytes 3538944 | tf_op jit(solution)/shard_map/all_to_all | solution.py:585
  289.4 4.5 %copy-start.3 = (bf16[8,48,384]{2,1,0:T(8,128)(2,1)S(1)}, bf16[8,48,384]{2,1,0:T(8,128)(2,1)}, u32[]{:S(2)}) copy-start(bf16[8,48,384]{2,1,0:T(8,128)(2,1)} %first_half.1.refs_5_.refs_0_) | copy-start | bytes 884740
  292.4 31.3 %collective-permute-start.6 = (bf16[10,48,384]{2,1,0:T(8,128)(2,1)}, bf16[10,48,384]{2,1,0:T(8,128)(2,1)S(1)}, u32[]{:S(2)}, u32[]{:S(2)}) collective-permute-start(bf16[10,48,384]{2,1,0:T(8,128)(2,1)} %get-tuple-element.77), channel_id=1, source_target_pairs={{0,1},{1,0},{2,3},{3,2},{4,5},{5,4},{6,7},{7,6},{8,9},{9,8},{10,11... | collective-permute-start | bytes 1105928 | tf_op jit(solution)/shard_map/ppermute | solution.py:558
  293.9 16.2 %collective-permute-start.4 = (bf16[8,48,384]{2,1,0:T(8,128)(2,1)S(1)}, bf16[8,48,384]{2,1,0:T(8,128)(2,1)S(1)}, u32[]{:S(2)}, u32[]{:S(2)}) collective-permute-start(bf16[8,48,384]{2,1,0:T(8,128)(2,1)S(1)} %copy-done.3), channel_id=1, source_target_pairs={{0,3},{1,2},{2,1},{3,0},{4,7},{5,6},{6,5},{7,4},{8,11},{9,10},{10,... | collective-permute-start | bytes 884744 | tf_op jit(solution)/shard_map/ppermute | solution.py:558
  310.1 0.7 copy-start.13
  323.7 0.7 copy-start.10
  326.3 28.4 %collective-permute-start.7 = (bf16[10,48,384]{2,1,0:T(8,128)(2,1)}, bf16[10,48,384]{2,1,0:T(8,128)(2,1)S(1)}, u32[]{:S(2)}, u32[]{:S(2)}) collective-permute-start(bf16[10,48,384]{2,1,0:T(8,128)(2,1)} %second_half.1.refs_0_.refs_3_), channel_id=1, source_target_pairs={{0,3},{1,2},{2,1},{3,0},{4,7},{5,6},{6,5},{7,4},{8,11},{9,10},{10,... | collective-permute-start | bytes 1105928 | tf_op jit(solution)/shard_map/ppermute | solution.py:558
  331.4 26.0 %copy-start.2 = (bf16[8,48,384]{2,1,0:T(8,128)(2,1)S(1)}, bf16[8,48,384]{2,1,0:T(8,128)(2,1)}, u32[]{:S(2)}) copy-start(bf16[8,48,384]{2,1,0:T(8,128)(2,1)} %first_rest.1.refs_21_.refs_1_) | copy-start | bytes 884740
  331.4 28.1 %copy-start.22 = (s32[48]{0:T(128)S(1)}, s32[48]{0:T(128)}, u32[]{:S(2)}) copy-start(s32[48]{0:T(128)} %param.15) | copy-start | bytes 580
  331.4 28.1 %copy-start.23 = (s32[48]{0:T(128)S(1)}, s32[48]{0:T(128)}, u32[]{:S(2)}) copy-start(s32[48]{0:T(128)} %constant.107.clone) | copy-start | bytes 580
  331.4 11.6 %collective-permute-start.9 = (bf16[6,48,384]{2,1,0:T(8,128)(2,1)}, bf16[6,48,384]{2,1,0:T(8,128)(2,1)S(1)}, u32[]{:S(2)}, u32[]{:S(2)}) collective-permute-start(bf16[6,48,384]{2,1,0:T(8,128)(2,1)} %get-tuple-element.79), channel_id=1, source_target_pairs={{0,1},{1,0},{2,3},{3,2},{4,5},{5,4},{6,7},{7,6},{8,9},{9,8},{10,11... | collective-permute-start | bytes 663560 | tf_op jit(solution)/shard_map/ppermute | solution.py:558
  333.1 15.0 %collective-permute-start.12 = (f32[16,768]{1,0:T(8,128)}, f32[16,768]{1,0:T(8,128)S(1)}, u32[]{:S(2)}, u32[]{:S(2)}) collective-permute-start(f32[16,768]{1,0:T(8,128)} %pack.1), channel_id=1, source_target_pairs={{0,4},{4,0},{8,12},{12,8},{16,20},{20,16},{24,28},{28,24},{1,5},{5... | collective-permute-start | bytes 147464 | tf_op jit(solution)/shard_map/ppermute | solution.py:553
  343.0 0.7 copy-start.15
  345.5 28.7 %collective-permute-start.10 = (bf16[6,48,384]{2,1,0:T(8,128)(2,1)}, bf16[6,48,384]{2,1,0:T(8,128)(2,1)S(1)}, u32[]{:S(2)}, u32[]{:S(2)}) collective-permute-start(bf16[6,48,384]{2,1,0:T(8,128)(2,1)} %third_half.1.refs_0_), channel_id=1, source_target_pairs={{0,3},{1,2},{2,1},{3,0},{4,7},{5,6},{6,5},{7,4},{8,11},{9,10},{10,... | collective-permute-start | bytes 663560 | tf_op jit(solution)/shard_map/ppermute | solution.py:558
  348.9 4.1 collective-permute-start.13
  353.0 6.5 %collective-permute-start.14 = (f32[16,768]{1,0:T(8,128)S(1)}, f32[16,768]{1,0:T(8,128)S(1)}, u32[]{:S(2)}, u32[]{:S(2)}) collective-permute-start(f32[16,768]{1,0:T(8,128)S(1)} %add.92), channel_id=1, source_target_pairs={{0,16},{4,20},{8,24},{12,28},{16,0},{20,4},{24,8},{28,12},{1,17},{... | collective-permute-start | bytes 147464 | tf_op jit(solution)/shard_map/ppermute | solution.py:553
  354.7 0.7 copy-start.8
  357.4 22.7 %collective-permute-start.8 = (bf16[10,48,384]{2,1,0:T(8,128)(2,1)}, bf16[10,48,384]{2,1,0:T(8,128)(2,1)S(1)}, u32[]{:S(2)}, u32[]{:S(2)}) collective-permute-start(bf16[10,48,384]{2,1,0:T(8,128)(2,1)} %second_rest.1.refs_3_), channel_id=1, source_target_pairs={{0,1},{1,0},{2,3},{3,2},{4,5},{5,4},{6,7},{7,6},{8,9},{9,8},{10,11... | collective-permute-start | bytes 1105928 | tf_op jit(solution)/shard_map/ppermute | solution.py:558
  357.4 22.7 %collective-permute-start.5 = (bf16[8,48,384]{2,1,0:T(8,128)(2,1)S(1)}, bf16[8,48,384]{2,1,0:T(8,128)(2,1)S(1)}, u32[]{:S(2)}, u32[]{:S(2)}) collective-permute-start(bf16[8,48,384]{2,1,0:T(8,128)(2,1)S(1)} %copy-done.2), channel_id=1, source_target_pairs={{0,1},{1,0},{2,3},{3,2},{4,5},{5,4},{6,7},{7,6},{8,9},{9,8},{10,11... | collective-permute-start | bytes 884744 | tf_op jit(solution)/shard_map/ppermute | solution.py:558
  359.5 14.6 %collective-permute-start.15 = (f32[16,768]{1,0:T(8,128)S(1)}, f32[16,768]{1,0:T(8,128)S(1)}, u32[]{:S(2)}, u32[]{:S(2)}) collective-permute-start(f32[16,768]{1,0:T(8,128)S(1)} %add.93), channel_id=1, source_target_pairs={{0,1},{1,0},{2,3},{3,2},{4,5},{5,4},{6,7},{7,6},{8,9},{9,8},{10,11... | collective-permute-start | bytes 147464 | tf_op jit(solution)/shard_map/ppermute | solution.py:558
  374.1 5.4 %collective-permute-start.16 = (f32[16,768]{1,0:T(8,128)S(1)}, f32[16,768]{1,0:T(8,128)S(1)}, u32[]{:S(2)}, u32[]{:S(2)}) collective-permute-start(f32[16,768]{1,0:T(8,128)S(1)} %add.94), channel_id=1, source_target_pairs={{0,2},{1,3},{2,0},{3,1},{4,6},{5,7},{6,4},{7,5},{8,10},{9,11},{10,... | collective-permute-start | bytes 147464 | tf_op jit(solution)/shard_map/ppermute | solution.py:558
  374.2 0.7 copy-start.14
  376.6 6.1 %collective-permute-start.11 = (bf16[6,48,384]{2,1,0:T(8,128)(2,1)}, bf16[6,48,384]{2,1,0:T(8,128)(2,1)S(1)}, u32[]{:S(2)}, u32[]{:S(2)}) collective-permute-start(bf16[6,48,384]{2,1,0:T(8,128)(2,1)} %third_rest.1.refs_5_), channel_id=1, source_target_pairs={{0,1},{1,0},{2,3},{3,2},{4,5},{5,4},{6,7},{7,6},{8,9},{9,8},{10,11... | collective-permute-start | bytes 663560 | tf_op jit(solution)/shard_map/ppermute | solution.py:558
  380.1 2.7 copy-start.12
  380.1 2.7 copy-start.9
  382.8 0.7 copy-start.16
  387.1 3.8 copy-start.7
  387.1 4.3 %copy-start.18 = (f32[9216]{0:T(1024)S(1)}, f32[9216]{0:T(1024)}, u32[]{:S(2)}) copy-start(f32[9216]{0:T(1024)} %param.17) | copy-start | bytes 110596
  387.1 4.3 %copy-start.20 = (f32[9216]{0:T(1024)S(1)}, f32[9216]{0:T(1024)}, u32[]{:S(2)}) copy-start(f32[9216]{0:T(1024)} %param.18) | copy-start | bytes 110596
  387.1 26.8 %all-to-all-start.2 = ((bf16[8,6,48,384]{3,2,1,0:T(8,128)(2,1)}), bf16[8,6,48,384]{3,2,1,0:T(8,128)(2,1)S(1)}, u32[]{:S(2)}, u32[]{:S(2)}) async-start(bf16[8,6,48,384]{3,2,1,0:T(8,128)(2,1)} %lay.1), calls=%async_computation.3 | async-start | bytes 3538944 | tf_op jit(solution)/shard_map/all_to_all | solution.py:887
  390.9 31.2 %copy-start.19 = (f32[9216]{0:T(1024)}, f32[9216]{0:T(1024)S(1)}, u32[]{:S(2)}) copy-start(f32[9216]{0:T(1024)S(1)} %reshape.56) | copy-start | bytes 110596
  413.9 1.2 copy-start.1
Sparse Core Ops, SparseCore 0:
  11.7 105.9 all-gather.2
  119.8 38.4 all-gather.4
  182.9 52.0 reduce-scatter.1

commit v3 on v2

--- a/solution.py
+++ b/solution.py
@@ -71,8 +71,9 @@
             ][0]
 
 
-def call(kernel, grid, ins, outs, scratch=(), scalars=(), ties=(), name=None):
+def call(kernel, grid, ins, outs, scratch=(), scalars=(), ties=(), onto=(), name=None):
     first = len(scalars) + len(ins)
+    ties = list(onto) + list(ties)
 
     def body(*refs):
         kernel(*refs[:first], *refs[first + len(ties) :])
@@ -93,6 +94,7 @@
             dimension_semantics=("arbitrary",) * len(grid), vmem_limit_bytes=VMEM
         ),
         cost_estimate=pl.CostEstimate(flops=1024, bytes_accessed=1024, transcendentals=0),
+        input_output_aliases={first + place: place for place in range(len(onto))},
         name=name,
     )(*scalars, *[array for array, _, _ in ins], *ties)
 
@@ -241,6 +243,17 @@
     return jnp.where(cols == head, values, jnp.zeros_like(values))
 
 
+def staged(bodies, stages, lags):
+    held = [None] * len(bodies)
+    for step in range(len(bodies) + sum(lags)):
+        at = step
+        for index, stage in enumerate(stages):
+            if 0 <= at < len(bodies):
+                held[at] = stage(*bodies[at]) if index == 0 else stage(held[at], *bodies[at])
+            if index < len(lags):
+                at -= lags[index]
+
+
 def attend_kernel(lengths_ref, q_ref, k_ref, v_ref, out_ref, lse_ref, bias, mixed, *, row, docs):
     seq_len = q_ref.shape[0]
 
@@ -250,18 +263,27 @@
 
     query_t = (q_ref[...] * BF(HEAD_DIM**-0.5)).T
     value_t = v_ref[...].T
-    for head in range(2):
+    query_h = [head_rows(query_t, head) for head in range(2)]
+
+    def scores_of(head, first, low, high, start):
+        cols = slice(first, first + TILE)
+        scores = nn(k_ref[low:high, :], query_h[head][:, cols]) + bias[start : start + high - low, :]
+        return scores, jnp.max(scores, axis=0, keepdims=True)
+
+    def weights_of(held, head, first, low, high, start):
+        scores, peak = held
+        weights = jnp.exp(scores - peak)
+        total = jnp.sum(weights, axis=0, keepdims=True)
+        lse_ref[0, head : head + 1, first : first + TILE] = peak + jnp.log(total)
+        return weights.astype(BF), 1.0 / total
+
+    def mix(held, head, first, low, high, start):
+        weights, scale = held
         rows = slice(head * HEAD_DIM, (head + 1) * HEAD_DIM)
-        query_h = head_rows(query_t, head)
-        for first, low, high, start in spans(seq_len)[0]:
-            cols = slice(first, first + TILE)
-            scores = nn(k_ref[low:high, :], query_h[:, cols]) + bias[start : start + high - low, :]
-            peak = jnp.max(scores, axis=0, keepdims=True)
-            weights = jnp.exp(scores - peak)
-            total = jnp.sum(weights, axis=0, keepdims=True)
-            part = nn(value_t[rows, low:high], weights.astype(BF))
-            mixed[rows, cols] = part / total
-            lse_ref[0, head : head + 1, cols] = peak + jnp.log(total)
+        mixed[rows, first : first + TILE] = nn(value_t[rows, low:high], weights) * scale
+
+    bodies = [(head,) + span for head in range(2) for span in spans(seq_len)[0]]
+    staged(bodies, (scores_of, weights_of, mix), (2, 1))
     out_ref[...] = mixed[...].astype(BF).T
 
 
@@ -298,22 +320,43 @@
     weighted = grad_t.astype(F32) * out_ref[...].T.astype(F32)
     key_sum[...] = jnp.zeros_like(key_sum)
     value_sum[...] = jnp.zeros_like(value_sum)
-    for head in range(2):
-        rows = slice(head * HEAD_DIM, (head + 1) * HEAD_DIM)
-        query_th = head_rows(query_t, head)
-        grad_th = head_rows(grad_t, head)
-        query_h = head_cols(query, head)
-        grad_h = head_cols(grad, head)
-        inner = jnp.sum(weighted[rows, :], axis=0, keepdims=True)
-        for first, low, high, start in spans(seq_len)[0]:
-            cols = slice(first, first + TILE)
-            scores = nn(k_ref[low:high, :], query_th[:, cols]) + bias[start : start + high - low, :]
-            probs = jnp.exp(scores - lse_ref[0, head : head + 1, cols])
-            grad_probs = nn(v_ref[low:high, :], grad_th[:, cols])
-            grad_scores = (probs * (grad_probs - inner[:, cols])).astype(BF)
-            value_sum[low:high, :] += nn(probs.astype(BF), grad_h[cols, :])
-            key_sum[low:high, :] += nn(grad_scores, query_h[cols, :])
-            query_sum[rows, cols] = nn(key_t[rows, low:high], grad_scores)
+    query_th = [head_rows(query_t, head) for head in range(2)]
+    grad_th = [head_rows(grad_t, head) for head in range(2)]
+    query_h = [head_cols(query, head) for head in range(2)]
+    grad_h = [head_cols(grad, head) for head in range(2)]
+    inner = [
+        col_sum(weighted[head * HEAD_DIM : (head + 1) * HEAD_DIM, :]) for head in range(2)
+    ]
+    bodies = []
+    for first, low, high, start in spans(seq_len)[0]:
+        for head in range(2):
+            for key in range(low, high, TILE):
+                bodies.append((head, first, key, start + key - low, key == low))
+
+    def products(head, first, key, start, opening):
+        cols, rows = slice(first, first + TILE), slice(key, key + TILE)
+        scores = nn(k_ref[rows, :], query_th[head][:, cols]) + bias[start : start + TILE, :]
+        return scores, nn(v_ref[rows, :], grad_th[head][:, cols])
+
+    def score_grads(held, head, first, key, start, opening):
+        scores, grad_probs = held
+        cols = slice(first, first + TILE)
+        probs = jnp.exp(scores - lse_ref[0, head : head + 1, cols])
+        return probs.astype(BF), (probs * (grad_probs - inner[head][:, cols])).astype(BF)
+
+    def add_grads(held, head, first, key, start, opening):
+        probs, grad_scores = held
+        cols, rows = slice(first, first + TILE), slice(key, key + TILE)
+        value_sum[rows, :] += nn(probs, grad_h[head][cols, :])
+        key_sum[rows, :] += nn(grad_scores, query_h[head][cols, :])
+        lanes = slice(head * HEAD_DIM, (head + 1) * HEAD_DIM)
+        part = nn(key_t[lanes, rows], grad_scores)
+        if opening:
+            query_sum[lanes, cols] = part
+        else:
+            query_sum[lanes, cols] += part
+
+    staged(bodies, (products, score_grads, add_grads), (2, 1))
     dq_ref[...] = (query_sum[...] * (HEAD_DIM**-0.5)).astype(BF).T
     dk_ref[...] = key_sum[...].astype(BF)
     dv_ref[...] = value_sum[...].astype(BF)
@@ -363,12 +406,10 @@
     else:
         mlp_ref, back_ref, grad_ref, bias_ref = refs[:4]
         refs = refs[4:]
-    w_fc, w_fc_t, w_proj, w_proj_t, hidden, grad_pre, whole_grad = refs
+    w_fc, w_proj, hidden, grad_pre, whole_grad = refs
     step = pl.program_id(0)
     place(w_fc, fc_blocks, 2, 2)
     place(w_proj, proj_blocks, 2, 2)
-    w_fc_t[...] = w_fc[...].T
-    w_proj_t[...] = w_proj[...].T
     bias_row = vec_ref[pl.ds(FC_BIAS + first + step, 1)]
 
     @pl.when(step == 0)
@@ -380,10 +421,11 @@
             mlp_ref[...] = before[0][...]
             back_ref[...] = before[1][...]
 
-    def chunk(index, total):
-        rows = pl.ds(pl.multiple_of(index * TILE, TILE), TILE)
-        pre = nn(normed_ref[rows], w_fc[...]) + bias_row
-        grad = nn(cot_ref[rows], w_proj_t[...])
+    def entering(rows):
+        return nn(normed_ref[rows], w_fc[...]) + bias_row, nt(cot_ref[rows], w_proj[...])
+
+    def activated(held, rows):
+        pre, grad = held
         root = 0.7978845608028654
         square = pre * pre
         tanh = jnp.tanh(pre * (root + root * 0.044715 * square))
@@ -394,11 +436,15 @@
         hidden[rows] = low
         grad_pre[rows] = back
         mlp_ref[rows] += nn(low, w_proj[...])
-        back_ref[rows] += nn(back, w_fc_t[...])
-        return total + col_sum(back.astype(F32))
-
+        back_ref[rows] += nt(back, w_fc[...])
+        sums.append(col_sum(back.astype(F32)))
+
+    sums = []
     count = normed_ref.shape[0]
-    bias_ref[0] = lax.fori_loop(0, count // TILE, chunk, jnp.zeros((1, D), F32))
+    staged(
+        [(slice(row, row + TILE),) for row in range(0, count, TILE)], (entering, activated), (1,)
+    )
+    bias_ref[0] = sum(sums)
     for base, left, right in ((0, normed_ref, grad_pre), (4, hidden, cot_ref)):
         if paired:
             whole_grad[...] = tn(left[...], right[...])
@@ -585,9 +631,13 @@
     return lax.all_to_all(values, "dp", 0, 0, axis_index_groups=groups, tiled=True)
 
 
-def everywhere_sum(values, bits):
-    for bit in range(bits):
+def dp_sum(values):
+    for bit in range(lax.axis_size("dp").bit_length() - 1):
         values = values + across_dp(values, bit)
+    return values
+
+
+def fsdp_sum(values):
     offset = 1
     while offset < lax.axis_size("fsdp"):
         values = values + across_fsdp(values, offset)
@@ -610,7 +660,6 @@
 ):
     dp_count = lax.axis_size("dp")
     fsdp_count = lax.axis_size("fsdp")
-    bits = dp_count.bit_length() - 1
     own_blocks, own_rows, width = matrices.shape
     blocks = own_blocks * dp_count
     height = width // dp_count
@@ -731,7 +780,7 @@
             [out_whole((count, D), F32), out_whole((count, D), F32)]
             + pieces
             + [((tiles, 1, D), F32, (1, 1, D), lambda t, *_: (t, 0, 0))],
-            [pltpu.VMEM((D, D), BF)] * 4
+            [pltpu.VMEM((D, D), BF)] * 2
             + [pltpu.VMEM((count, D), BF)] * 2
             + [pltpu.VMEM((D, D), F32)],
             scalars=[slot_place, me],
@@ -772,20 +821,19 @@
 
     second_core = core_sum([mlp_grads[1], out_grads], "second_core")
     first_halves = plane_sum(first_grads.reshape(1, -1, height, width), half, [], "first_split")
-    first_half = line_half(first_halves, [grad_attended], "first_half")
+    first_half = line_half(first_halves, [], "first_half")
     second_parts = plane_parts(second_core)
-    query_grads, key_grads, value_grads = [], [], []
-    for row in range(rows_here):
-        grads = call(
+    def attend_back(row, begin, stop, onto, ties):
+        return call(
             functools.partial(attend_back_kernel, row=row, docs=docs),
-            (pairs,),
-            [pair_in(projected, row, part * pairs) for part in range(3)]
+            (stop - begin,),
+            [pair_in(projected, row, part * pairs + begin) for part in range(3)]
             + [
-                pair_in(attended, row, 0),
-                pair_in(grad_attended, row, 0),
-                (lses[row], (1, 2, seq_len), lambda p, *_: (p, 0, 0)),
+                pair_in(attended, row, begin),
+                pair_in(grad_attended, row, begin),
+                (lses[row], (1, 2, seq_len), lambda p, *_: (p + begin, 0, 0)),
             ],
-            [((seq_len, D), BF, (seq_len, PAIR), lambda p, *_: (0, p))] * 3,
+            [((count, D), BF, (seq_len, PAIR), lambda p, *_: (row, p + begin))] * 3,
             [
                 pltpu.VMEM((bias_rows, TILE), F32),
                 pltpu.VMEM((seq_len, PAIR), F32),
@@ -793,15 +841,16 @@
                 pltpu.VMEM((PAIR, seq_len), F32),
             ],
             scalars=[doc_lengths],
-            ties=[second_core, first_halves[0]],
+            ties=ties,
+            onto=onto,
             name="attend_back",
         )
-        for kept, one in zip((query_grads, key_grads, value_grads), grads):
-            kept.append(one)
-    dq, dk, dv = [
-        kept[0] if rows_here == 1 else jnp.concatenate(kept, axis=0)
-        for kept in (query_grads, key_grads, value_grads)
-    ]
+
+    grads = ()
+    for row in range(rows_here):
+        grads = attend_back(row, 0, pairs // 2, grads, [second_core])
+        grads = attend_back(row, pairs // 2, pairs, grads, [first_halves[0]])
+    dq, dk, dv = grads
 
     half_shape = (pair_count, 12, height, width)
     keep, send, sums_qkv = call(
@@ -815,7 +864,6 @@
         ties=[first_half],
         name="qkv_weight_back",
     )
-    first_total = line_rest(first_half, [keep], "first_rest")
     third_core = core_sum([(keep, send)], "third_core")
     second_halves = plane_sum(second_parts, half, [], "second_plane")
     third_parts = plane_parts(third_core)
@@ -835,11 +883,12 @@
         [((count, D), F32, (TILE, D), lambda i, *_: (i, 0)), out_whole((8, D), F32)],
         [pltpu.VMEM((D, 3 * D), BF)],
         scalars=[slot_place],
-        ties=[second_halves[0], third_core, first_total],
+        ties=[second_halves[0], third_core],
         name="input_back",
     )
 
-    second_half = line_half(second_halves, [x_grad], "second_half")
+    first_total = line_rest(first_half, [x_grad], "first_rest")
+    second_half = line_half(second_halves, [x_grad, first_total], "second_half")
     second_total = line_rest(second_half, [], "second_rest")
     vector_local = call(
         pack_kernel,
@@ -848,7 +897,8 @@
         [out_whole((16, D), F32)],
         name="pack",
     )[0]
-    vector_sums = everywhere_sum(vector_local, bits)
+    vector_plane = dp_sum(vector_local)
+    vector_sums = fsdp_sum(vector_plane)
     third_halves = plane_sum(third_parts, half, [second_half], "third_plane")
     third_total = line_rest(line_half(third_halves, [], "third_half"), [], "third_rest")
     vector_grad = vector_sums[:12].reshape(-1)
@@ -881,7 +931,7 @@
         [out_whole((dp_count, own_blocks, height, width), BF)],
         [pltpu.VMEM((blocks, height, width), BF)],
         scalars=[source],
-        ties=[vector_sums],
+        ties=[vector_plane],
         name="lay",
     )[0]
     grad_whole = lax.all_to_all(laid, "dp", 0, 0, tiled=True)

time: 430 us -> 402 us (0.935)
  waiting for transfers between devices: 180 us -> 164 us
  Pallas kernels: 190 us -> 176 us
    pallas_call x23 -> x24, Pallas kernels: 190 us -> 176 us  [call(): pl.pallas_call(body, grid_spec=spec, out_shape=[jax.ShapeDtypeStruct(shap...]
    all_to_all x1, waiting for transfers between devices: 21.8 us -> 12.5 us  [per_device(): grad_whole = lax.all_to_all(laid, 'dp', 0, 0, tiled=True)]
    ppermute x11, waiting for transfers between devices: 43.1 us -> 36.9 us  [across_fsdp(): return lax.ppermute(values, 'fsdp', [(i, i ^ offset) for i in range(count)])]
  transfers between devices with their start and end apart: 23 -> 23, of which waited for: 10 -> 11; matrix products, arithmetic and copies ran while one was open for 1% -> 1% of each run, Pallas kernels for 42% -> 42%
where the time goes in v3:
time: 402 us; the launch traced here: 397 us
  Pallas kernels  176 us (44%)
  waiting for transfers between devices  164 us (41%)
  starting transfers between devices  26.5 us (7%)
  between operations  14.3 us (4%)
  local copies, waits for them, and re-layouts  10.2 us (3%)
  other arithmetic  6.67 us (2%)
    pallas_call x24, Pallas kernels, call(): pl.pallas_call(body, grid_spec=spec, out_shape=[jax.ShapeDtypeStruct(shap...  176 us
    all_gather x1, waiting for transfers between devices, per_device(): lax.all_gather(matrices.astype(BF), ('dp', 'fsdp'), axis=1, tiled=True)  106 us
    ppermute x11, waiting for transfers between devices, across_fsdp(): return lax.ppermute(values, 'fsdp', [(i, i ^ offset) for i in range(count)])  36.9 us
    all_to_all x1, waiting for transfers between devices, per_device(): grad_whole = lax.all_to_all(laid, 'dp', 0, 0, tiled=True)  12.5 us
    unnamed x48, local copies, waits for them, and re-layouts  9.53 us
    ppermute x11, starting transfers between devices, across_fsdp(): return lax.ppermute(values, 'fsdp', [(i, i ^ offset) for i in range(count)])  9.53 us
    all_to_all x2, starting transfers between devices, plane_parts(): lax.all_to_all(values, 'dp', 0, 0, axis_index_groups=groups, tiled=True)  8.57 us
    ppermute x6, waiting for transfers between devices, across_dp(): return lax.ppermute(values, 'dp', [(i, i ^ 1 << bit) for i in range(count)])  8.09 us
  transfers between devices with their start and end apart: 23, of which 11 were waited for; matrix products, arithmetic and copies ran while one was open for 1% of the time, Pallas kernels for 42%

profile of v3, /device:TPU:0, one launch (start us, length us, event | category | flops | bytes accessed | tf_op | source)
XLA Modules:
  0.0 397.1 jit_solution(2491572757237324161)
XLA Ops:
  7.3 2.0 convert_element_type.6
  9.4 0.8 convert_element_type.7
  11.4 106.2 %all-gather.3.cloned.1.call-done = bf16[6,3072,384]{2,1,0:T(8,128)(2,1)} async-done(((bf16[6,96,384]{2,1,0:T(8,128)(2,1)}), bf16[6,3072,384]{2,1,0:T(8,128)(2,1)}) %all-gather.3.cloned.1.call-update) | async-done | bytes 14155792 | tf_op jit(solution)/shard_map/all_gather | solution.py:672
  117.7 9.7 %qkv.1 = (bf16[1024,768]{1,0:T(8,128)(2,1)}, bf16[1024,2304]{1,0:T(8,128)(2,1)}) custom-call(s32[48]{0:T(128)} %fusion.5.refs_0_, bf16[1024,768]{1,0:T(8,128)(2,1)} %refs_1_.3, f32[12,768]{1,0:T(8,128)} %reshape.50.refs_2_.refs_3_.refs_4_.refs_7_.refs_6_, bf16[48,384,384]{2,1,0:T(8,128)(2,1)} %bitcast.9, bf16[48,384,384]{2,1,0:T(8,128)(2,1)} %bitcast.10, ...), custom_call_target="tpu_custom_call" | custom-call | flops 1024 | bytes 1024 | tf_op jit(solution)/shard_map/qkv/pallas_call | solution.py:89
  127.4 14.0 %attend.1 = (bf16[1024,768]{1,0:T(8,128)(2,1)}, f32[6,2,1024]{2,1,0:T(2,128)}) custom-call(s32[1,8]{1,0:T(1,128)} %refs_0_.5, bf16[1024,2304]{1,0:T(8,128)(2,1)} %get-tuple-element.53.refs_1_.refs_2_.refs_3_, bf16[1024,2304]{1,0:T(8,128)(2,1)} %get-tuple-element.53.refs_1_.refs_2_.refs_3_, bf16[1024,2304]{1,0:T(8,128)(2,1)} %get-tuple-element.53.refs_1_.refs_2_.refs_3_), custom_call_target="tpu_custom_call" | custom-call | flops 1024 | bytes 1024 | tf_op jit(solution)/shard_map/attend/pallas_call | solution.py:89
  141.4 6.8 %attn_out.1 = (f32[1024,768]{1,0:T(8,128)}, bf16[1024,768]{1,0:T(8,128)(2,1)}, f32[8,768]{1,0:T(8,128)}) custom-call(s32[48]{0:T(128)} %fusion.5.refs_0_, bf16[1024,768]{1,0:T(8,128)(2,1)} %get-tuple-element.54.refs_1_.refs_6_.refs_4_, bf16[1024,768]{1,0:T(8,128)(2,1)} %refs_1_.3, f32[12,768]{1,0:T(8,128)} %reshape.50.refs_2_.refs_3_.refs_4_.refs_7_.refs_6_, ...), custom_call_target="tpu_custom_call" | custom-call | flops 1024 | bytes 1024 | tf_op jit(solution)/shard_map/attn_out/pallas_call | solution.py:89
  148.3 22.3 %mlp.2 = (f32[1024,768]{1,0:T(8,128)}, f32[1024,768]{1,0:T(8,128)}, bf16[8,2,8,48,384]{4,3,2,1,0:T(8,128)(2,1)}, f32[2,1,768]{2,1,0:T(1,128)}) custom-call(s32[48]{0:T(128)} %fusion.5.refs_0_, s32[1]{0:T(128)} %bitcast.refs_1_.refs_0_, bf16[1024,768]{1,0:T(8,128)(2,1)} %get-tuple-element.56.refs_2_, bf16[1024,768]{1,0:T(8,128)(2,1)} %refs_5_.2, ...), custom_call_target="tpu_custom_call" | custom-call | flops 1024 | bytes 1024 | tf_op jit(solution)/shard_map/mlp/pallas_call | solution.py:89
  170.6 26.3 %mlp.3 = (f32[1024,768]{1,0:T(8,128)}, f32[1024,768]{1,0:T(8,128)}, bf16[4,16,48,384]{3,2,1,0:T(8,128)(2,1)}, bf16[4,16,48,384]{3,2,1,0:T(8,128)(2,1)}, f32[2,1,768]{2,1,0:T(1,128)}) custom-call(s32[48]{0:T(128)} %fusion.5.refs_0_, s32[1]{0:T(128)} %bitcast.refs_1_.refs_0_, bf16[1024,768]{1,0:T(8,128)(2,1)} %get-tuple-element.56.refs_2_, ...), custom_call_target="tpu_custom_call" | custom-call | flops 1024 | bytes 1024 | tf_op jit(solution)/shard_map/mlp/pallas_call | solution.py:89
  197.2 13.1 %middle_back.1 = (bf16[1024,768]{1,0:T(8,128)(2,1)}, f32[1024,768]{1,0:T(8,128)}, bf16[1024,768]{1,0:T(8,128)(2,1)}, bf16[4,4,48,384]{3,2,1,0:T(8,128)(2,1)}, bf...) custom-call(s32[48]{0:T(128)} %fusion.5.refs_0_, s32[1]{0:T(128)} %bitcast.refs_1_.refs_0_, ...), custom_call_target="tpu_custom_call" | custom-call | flops 1024 | bytes 1024 | tf_op jit(solution)/shard_map/middle_back/pallas_call | solution.py:89
  210.5 2.0 collective-permute-done.1.refs_3_
  213.3 0.9 copy-done.4
  214.2 4.9 %second_core.1.refs_7_ = bf16[4,20,48,384]{3,2,1,0:T(8,128)(2,1)} custom-call(bf16[4,16,48,384]{3,2,1,0:T(8,128)(2,1)} %get-tuple-element.64.refs_0_, bf16[4,16,48,384]{3,2,1,0:T(8,128)(2,1)} %copy-done.4, bf16[4,4,48,384]{3,2,1,0:T(8,128)(2,1)} %get-tuple-element.66.refs_2_, bf16[4,4,48,384]{3,2,1,0:T(8,128)(2,1)} %copy-done.6), custom_call_target="tpu_custom_call" | custom-call | flops 1024 | bytes 1024 | tf_op jit(solution)/shard_map/second_core/pallas_call | solution.py:89
  219.1 3.9 all-to-all-start
  223.1 1.9 first_split.1
  225.0 1.3 collective-permute-start.2
  226.2 12.1 %attend_back.2 = (bf16[1024,768]{1,0:T(8,128)(2,1)}, bf16[1024,768]{1,0:T(8,128)(2,1)}, bf16[1024,768]{1,0:T(8,128)(2,1)}) custom-call(s32[1,8]{1,0:T(1,128)} %refs_0_.5, bf16[1024,2304]{1,0:T(8,128)(2,1)} %get-tuple-element.53.refs_1_.refs_2_.refs_3_, bf16[1024,2304]{1,0:T(8,128)(2,1)} %get-tuple-element.53.refs_1_.refs_2_.refs_3_, ...), custom_call_target="tpu_custom_call" | custom-call | flops 1024 | bytes 1024 | tf_op jit(solution)/shard_map/attend_back/pallas_call | solution.py:89
  238.4 12.1 %attend_back.3 = (bf16[1024,768]{1,0:T(8,128)(2,1)}, bf16[1024,768]{1,0:T(8,128)(2,1)}, bf16[1024,768]{1,0:T(8,128)(2,1)}) custom-call(s32[1,8]{1,0:T(1,128)} %refs_0_.5, bf16[1024,2304]{1,0:T(8,128)(2,1)} %get-tuple-element.53.refs_1_.refs_2_.refs_3_, ...), custom_call_target="tpu_custom_call", output_to_operand_aliasing={{0}: (7, {}), {1}: (8, {}), {2}: (9, {})} | custom-call | flops 1024 | bytes 1024 | tf_op jit(solution)/shard_map/attend_back/pallas_call | solution.py:89
  251.2 1.8 first_half.1.refs_5_.refs_0_
  253.1 8.6 %qkv_weight_back.1 = (bf16[4,12,48,384]{3,2,1,0:T(8,128)(2,1)}, bf16[4,12,48,384]{3,2,1,0:T(8,128)(2,1)}, f32[8,768]{1,0:T(8,128)}) custom-call(s32[1]{0:T(128)} %bitcast.refs_1_.refs_0_, bf16[1024,768]{1,0:T(8,128)(2,1)} %get-tuple-element.78.refs_1_, bf16[1024,768]{1,0:T(8,128)(2,1)} %get-tuple-element.73.refs_2_, ...), custom_call_target="tpu_custom_call" | custom-call | flops 1024 | bytes 1024 | tf_op jit(solution)/shard_map/qkv_weight_back/pallas_call | solution.py:89
  261.8 4.0 %collective-permute-done.3.refs_1_ = bf16[4,12,48,384]{3,2,1,0:T(8,128)(2,1)} collective-permute-done((bf16[4,12,48,384]{3,2,1,0:T(8,128)(2,1)}, bf16[4,12,48,384]{3,2,1,0:T(8,128)(2,1)}, u32[]{:S(2)}, u32[]{:S(2)}) %collective-permute-start.3) | collective-permute-done | bytes 1769504 | tf_op jit(solution)/shard_map/ppermute | solution.py:599
  265.8 4.1 %third_core.1.refs_20_ = bf16[4,12,48,384]{3,2,1,0:T(8,128)(2,1)} custom-call(bf16[4,12,48,384]{3,2,1,0:T(8,128)(2,1)} %get-tuple-element.80.refs_0_, bf16[4,12,48,384]{3,2,1,0:T(8,128)(2,1)} %collective-permute-done.3.refs_1_), custom_call_target="tpu_custom_call" | custom-call | flops 1024 | bytes 1024 | tf_op jit(solution)/shard_map/third_core/pallas_call | solution.py:89
  269.9 1.6 copy-done
  271.5 4.7 %all-to-all-start.1 = ((bf16[4,12,48,384]{3,2,1,0:T(8,128)(2,1)}), bf16[4,12,48,384]{3,2,1,0:T(8,128)(2,1)}, u32[]{:S(2)}, u32[]{:S(2)}) async-start(bf16[4,12,48,384]{3,2,1,0:T(8,128)(2,1)} %third_core.1.refs_20_), calls=%async_computation.2 | async-start | bytes 3538944 | tf_op jit(solution)/shard_map/all_to_all | solution.py:631
  276.2 3.0 second_plane.1
  279.9 3.1 collective-permute-start.4
  283.1 11.2 %input_back.1 = (f32[1024,768]{1,0:T(8,128)}, f32[8,768]{1,0:T(8,128)}) custom-call(s32[48]{0:T(128)} %fusion.5.refs_0_, bf16[1024,768]{1,0:T(8,128)(2,1)} %refs_1_.3, bf16[1024,768]{1,0:T(8,128)(2,1)} %get-tuple-element.73.refs_2_, bf16[1024,768]{1,0:T(8,128)(2,1)} %get-tuple-element.74.refs_3_, bf16[1024,768]{1,0:T(8,128)(2,1)} %get-tuple-element.75.refs_4_, ...), custom_call_target="tpu_custom_call" | custom-call | flops 1024 | bytes 1024 | tf_op jit(solution)/shard_map/input_back/pallas_call | solution.py:89
  294.2 4.0 collective-permute-done.4.refs_1_
  298.9 1.8 first_rest.1.refs_3_.refs_1_
  301.5 1.9 second_half.1.refs_0_.refs_3_
  304.1 2.3 third_plane.1
  306.5 13.5 %collective-permute-done.9.refs_1_ = bf16[6,48,384]{2,1,0:T(8,128)(2,1)S(1)} collective-permute-done((bf16[6,48,384]{2,1,0:T(8,128)(2,1)}, bf16[6,48,384]{2,1,0:T(8,128)(2,1)S(1)}, u32[]{:S(2)}, u32[]{:S(2)}) %collective-permute-start.9) | collective-permute-done | bytes 221216 | tf_op jit(solution)/shard_map/ppermute | solution.py:604
  320.8 1.8 third_half.1.refs_0_
  323.2 1.6 pack.1
  325.6 1.9 second_rest.1.refs_3_
  327.9 1.6 collective-permute-start.5
  330.3 1.9 collective-permute-start.13
  332.3 2.1 collective-permute-done.13
  334.4 2.0 collective-permute-start.14
  337.1 1.8 third_rest.1.refs_5_
  340.1 6.2 %collective-permute-done.5.refs_2_ = bf16[8,48,384]{2,1,0:T(8,128)(2,1)S(1)} collective-permute-done((bf16[8,48,384]{2,1,0:T(8,128)(2,1)S(1)}, bf16[8,48,384]{2,1,0:T(8,128)(2,1)S(1)}, u32[]{:S(2)}, u32[]{:S(2)}) %collective-permute-start.5) | collective-permute-done | bytes 294944 | tf_op jit(solution)/shard_map/ppermute | solution.py:604
  346.3 4.7 %collective-permute-done.11.refs_6_ = bf16[6,48,384]{2,1,0:T(8,128)(2,1)S(1)} collective-permute-done((bf16[6,48,384]{2,1,0:T(8,128)(2,1)}, bf16[6,48,384]{2,1,0:T(8,128)(2,1)S(1)}, u32[]{:S(2)}, u32[]{:S(2)}) %collective-permute-start.11) | collective-permute-done | bytes 221216 | tf_op jit(solution)/shard_map/ppermute | solution.py:604
  351.7 3.6 lay.1
  355.3 3.7 all-to-all-start.2
  359.1 4.1 %collective-permute-done.15 = f32[16,768]{1,0:T(8,128)S(1)} collective-permute-done((f32[16,768]{1,0:T(8,128)S(1)}, f32[16,768]{1,0:T(8,128)S(1)}, u32[]{:S(2)}, u32[]{:S(2)}) %collective-permute-start.15) | collective-permute-done | bytes 49184 | tf_op jit(solution)/shard_map/ppermute | solution.py:604
  364.0 4.5 %collective-permute-done.16 = f32[16,768]{1,0:T(8,128)S(1)} collective-permute-done((f32[16,768]{1,0:T(8,128)S(1)}, f32[16,768]{1,0:T(8,128)S(1)}, u32[]{:S(2)}, u32[]{:S(2)}) %collective-permute-start.16) | collective-permute-done | bytes 49184 | tf_op jit(solution)/shard_map/ppermute | solution.py:604
  369.7 12.5 %all-to-all-done.2.refs_1_ = bf16[8,6,48,384]{3,2,1,0:T(8,128)(2,1)S(1)} async-done(((bf16[8,6,48,384]{3,2,1,0:T(8,128)(2,1)}), bf16[8,6,48,384]{3,2,1,0:T(8,128)(2,1)S(1)}, u32[]{:S(2)}, u32[]{:S(2)}) %all-to-all-start.2) | async-done | bytes 1769504 | tf_op jit(solution)/shard_map/all_to_all | solution.py:937
  382.1 1.2 copy-done.1
  383.4 6.9 %factor.1 = (f32[6,96,384]{2,1,0:T(8,128)}, f32[6,96,384]{2,1,0:T(8,128)}, f32[6,96,384]{2,1,0:T(8,128)}, f32[6,96,384]{2,1,0:T(8,128)}) custom-call(s32[1]{0:T(128)} %bitcast.5.refs_0_, bf16[8,6,48,384]{3,2,1,0:T(8,128)(2,1)} %copy-done.1, bf16[6,384,384]{2,1,0:T(8,128)(2,1)} %all-gather.5.cloned.1.call-done.refs_15_.refs_2_, f32[6,96,384]{2,1,0:T(8,128)} %refs_3_.5, ...), custom_call_target="tpu_custom_call" | custom-call | flops 1024 | bytes 1024 | tf_op jit(solution)/shard_map/factor/pallas_call | solution.py:89
  (87 shorter events, 14.7 us)
Async XLA Ops:
  7.2 2.2 copy-start.5
  7.2 3.1 copy-start.17
  7.2 3.7 copy-start.21
  7.2 110.5 %all-gather.3.cloned.1.call-start = ((), (), s32[]{:S(2)}) async-start(), calls=%async_computation.4 | async-start | bytes 14598144 | tf_op jit(solution)/shard_map/all_gather | solution.py:672
  9.3 161.3 %all-gather.5.cloned.1.call-start = ((), (), s32[]{:S(2)}) async-start(), calls=%async_computation.5 | async-start | bytes 2211840 | tf_op jit(solution)/shard_map/all_gather | solution.py:674
  10.2 212.8 %reduce-scatter.2.cloned.1.call-start = ((), (), s32[]{:S(2)}) async-start(), calls=%async_computation.6 | async-start | bytes 5308416 | tf_op jit(solution)/shard_map/reduce_scatter | solution.py:793
  196.9 15.6 %collective-permute-start = (bf16[4,16,48,384]{3,2,1,0:T(8,128)(2,1)}, bf16[4,16,48,384]{3,2,1,0:T(8,128)(2,1)S(1)}, u32[]{:S(2)}, u32[]{:S(2)}) collective-permute-start(bf16[4,16,48,384]{3,2,1,0:T(8,128)(2,1)} %get-tuple-element.65), channel_id=1, source_target_pairs={{0,4},{4,0},{8,12},{12,8},{16,20},{20,16},{24,28},{28,24},{1,5},{5... | collective-permute-start | bytes 7077896 | tf_op jit(solution)/shard_map/ppermute | solution.py:599
  210.2 2.3 collective-permute-start.1
  212.5 0.8 copy-start.6
  212.5 1.7 copy-start.4
  219.1 50.8 %all-to-all-start = ((bf16[4,20,48,384]{3,2,1,0:T(8,128)(2,1)}), bf16[4,20,48,384]{3,2,1,0:T(8,128)(2,1)S(1)}, u32[]{:S(2)}, u32[]{:S(2)}) async-start(bf16[4,20,48,384]{3,2,1,0:T(8,128)(2,1)} %second_core.1.refs_7_), calls=%async_computation.1 | async-start | bytes 5898240 | tf_op jit(solution)/shard_map/all_to_all | solution.py:631
  225.0 25.5 %collective-permute-start.2 = (bf16[8,48,384]{2,1,0:T(8,128)(2,1)}, bf16[8,48,384]{2,1,0:T(8,128)(2,1)S(1)}, u32[]{:S(2)}, u32[]{:S(2)}) collective-permute-start(bf16[8,48,384]{2,1,0:T(8,128)(2,1)} %get-tuple-element.79), channel_id=1, source_target_pairs={{0,1},{1,0},{2,3},{3,2},{4,5},{5,4},{6,7},{7,6},{8,9},{9,8},{10,11... | collective-permute-start | bytes 884744 | tf_op jit(solution)/shard_map/ppermute | solution.py:604
  250.5 0.7 copy-start.11
  261.7 4.1 %collective-permute-start.3 = (bf16[4,12,48,384]{3,2,1,0:T(8,128)(2,1)}, bf16[4,12,48,384]{3,2,1,0:T(8,128)(2,1)}, u32[]{:S(2)}, u32[]{:S(2)}) collective-permute-start(bf16[4,12,48,384]{3,2,1,0:T(8,128)(2,1)} %get-tuple-element.81), channel_id=1, source_target_pairs={{0,4},{4,0},{8,12},{12,8},{16,20},{20,16},{24,28},{28,24},{1,5},{5... | collective-permute-start | bytes 5308424 | tf_op jit(solution)/shard_map/ppermute | solution.py:599
  269.9 1.6 copy-start
  271.5 32.6 %all-to-all-start.1 = ((bf16[4,12,48,384]{3,2,1,0:T(8,128)(2,1)}), bf16[4,12,48,384]{3,2,1,0:T(8,128)(2,1)}, u32[]{:S(2)}, u32[]{:S(2)}) async-start(bf16[4,12,48,384]{3,2,1,0:T(8,128)(2,1)} %third_core.1.refs_20_), calls=%async_computation.2 | async-start | bytes 3538944 | tf_op jit(solution)/shard_map/all_to_all | solution.py:631
  276.2 3.7 copy-start.3
  279.2 21.6 %collective-permute-start.6 = (bf16[10,48,384]{2,1,0:T(8,128)(2,1)}, bf16[10,48,384]{2,1,0:T(8,128)(2,1)S(1)}, u32[]{:S(2)}, u32[]{:S(2)}) collective-permute-start(bf16[10,48,384]{2,1,0:T(8,128)(2,1)} %get-tuple-element.83), channel_id=1, source_target_pairs={{0,1},{1,0},{2,3},{3,2},{4,5},{5,4},{6,7},{7,6},{8,9},{9,8},{10,11... | collective-permute-start | bytes 1105928 | tf_op jit(solution)/shard_map/ppermute | solution.py:604
  279.9 18.3 %collective-permute-start.4 = (bf16[8,48,384]{2,1,0:T(8,128)(2,1)S(1)}, bf16[8,48,384]{2,1,0:T(8,128)(2,1)S(1)}, u32[]{:S(2)}, u32[]{:S(2)}) collective-permute-start(bf16[8,48,384]{2,1,0:T(8,128)(2,1)S(1)} %copy-done.3), channel_id=1, source_target_pairs={{0,3},{1,2},{2,1},{3,0},{4,7},{5,6},{6,5},{7,4},{8,11},{9,10},{10,... | collective-permute-start | bytes 884744 | tf_op jit(solution)/shard_map/ppermute | solution.py:604
  298.2 0.7 copy-start.13
  300.8 0.7 copy-start.10
  303.4 21.4 %collective-permute-start.7 = (bf16[10,48,384]{2,1,0:T(8,128)(2,1)}, bf16[10,48,384]{2,1,0:T(8,128)(2,1)S(1)}, u32[]{:S(2)}, u32[]{:S(2)}) collective-permute-start(bf16[10,48,384]{2,1,0:T(8,128)(2,1)} %second_half.1.refs_0_.refs_3_), channel_id=1, source_target_pairs={{0,3},{1,2},{2,1},{3,0},{4,7},{5,6},{6,5},{7,4},{8,11},{9,10},{10,... | collective-permute-start | bytes 1105928 | tf_op jit(solution)/shard_map/ppermute | solution.py:604
  306.5 21.4 %copy-start.2 = (bf16[8,48,384]{2,1,0:T(8,128)(2,1)S(1)}, bf16[8,48,384]{2,1,0:T(8,128)(2,1)}, u32[]{:S(2)}) copy-start(bf16[8,48,384]{2,1,0:T(8,128)(2,1)} %first_rest.1.refs_3_.refs_1_) | copy-start | bytes 884740
  306.5 25.7 %copy-start.22 = (s32[48]{0:T(128)S(1)}, s32[48]{0:T(128)}, u32[]{:S(2)}) copy-start(s32[48]{0:T(128)} %param.15) | copy-start | bytes 580
  306.5 25.7 %copy-start.23 = (s32[48]{0:T(128)S(1)}, s32[48]{0:T(128)}, u32[]{:S(2)}) copy-start(s32[48]{0:T(128)} %constant.107.clone) | copy-start | bytes 580
  306.5 13.6 %collective-permute-start.9 = (bf16[6,48,384]{2,1,0:T(8,128)(2,1)}, bf16[6,48,384]{2,1,0:T(8,128)(2,1)S(1)}, u32[]{:S(2)}, u32[]{:S(2)}) collective-permute-start(bf16[6,48,384]{2,1,0:T(8,128)(2,1)} %get-tuple-element.85), channel_id=1, source_target_pairs={{0,1},{1,0},{2,3},{3,2},{4,5},{5,4},{6,7},{7,6},{8,9},{9,8},{10,11... | collective-permute-start | bytes 663560 | tf_op jit(solution)/shard_map/ppermute | solution.py:604
  320.1 0.7 copy-start.15
  322.5 13.9 %collective-permute-start.10 = (bf16[6,48,384]{2,1,0:T(8,128)(2,1)}, bf16[6,48,384]{2,1,0:T(8,128)(2,1)S(1)}, u32[]{:S(2)}, u32[]{:S(2)}) collective-permute-start(bf16[6,48,384]{2,1,0:T(8,128)(2,1)} %third_half.1.refs_0_), channel_id=1, source_target_pairs={{0,3},{1,2},{2,1},{3,0},{4,7},{5,6},{6,5},{7,4},{8,11},{9,10},{10,... | collective-permute-start | bytes 663560 | tf_op jit(solution)/shard_map/ppermute | solution.py:604
  324.8 4.7 %collective-permute-start.12 = (f32[16,768]{1,0:T(8,128)}, f32[16,768]{1,0:T(8,128)S(1)}, u32[]{:S(2)}, u32[]{:S(2)}) collective-permute-start(f32[16,768]{1,0:T(8,128)} %pack.1), channel_id=1, source_target_pairs={{0,4},{4,0},{8,12},{12,8},{16,20},{20,16},{24,28},{28,24},{1,5},{5... | collective-permute-start | bytes 147464 | tf_op jit(solution)/shard_map/ppermute | solution.py:599
  324.8 0.7 copy-start.9
  327.5 18.8 %collective-permute-start.8 = (bf16[10,48,384]{2,1,0:T(8,128)(2,1)}, bf16[10,48,384]{2,1,0:T(8,128)(2,1)S(1)}, u32[]{:S(2)}, u32[]{:S(2)}) collective-permute-start(bf16[10,48,384]{2,1,0:T(8,128)(2,1)} %second_rest.1.refs_3_), channel_id=1, source_target_pairs={{0,1},{1,0},{2,3},{3,2},{4,5},{5,4},{6,7},{7,6},{8,9},{9,8},{10,11... | collective-permute-start | bytes 1105928 | tf_op jit(solution)/shard_map/ppermute | solution.py:604
  327.9 18.4 %collective-permute-start.5 = (bf16[8,48,384]{2,1,0:T(8,128)(2,1)S(1)}, bf16[8,48,384]{2,1,0:T(8,128)(2,1)S(1)}, u32[]{:S(2)}, u32[]{:S(2)}) collective-permute-start(bf16[8,48,384]{2,1,0:T(8,128)(2,1)S(1)} %copy-done.2), channel_id=1, source_target_pairs={{0,1},{1,0},{2,3},{3,2},{4,5},{5,4},{6,7},{7,6},{8,9},{9,8},{10,11... | collective-permute-start | bytes 884744 | tf_op jit(solution)/shard_map/ppermute | solution.py:604
  330.3 4.1 %collective-permute-start.13 = (f32[16,768]{1,0:T(8,128)S(1)}, f32[16,768]{1,0:T(8,128)S(1)}, u32[]{:S(2)}, u32[]{:S(2)}) collective-permute-start(f32[16,768]{1,0:T(8,128)S(1)} %add.91), channel_id=1, source_target_pairs={{0,8},{4,12},{8,0},{12,4},{16,24},{20,28},{24,16},{28,20},{1,9},{5... | collective-permute-start | bytes 147464 | tf_op jit(solution)/shard_map/ppermute | solution.py:599
  334.4 5.1 %collective-permute-start.14 = (f32[16,768]{1,0:T(8,128)S(1)}, f32[16,768]{1,0:T(8,128)S(1)}, u32[]{:S(2)}, u32[]{:S(2)}) collective-permute-start(f32[16,768]{1,0:T(8,128)S(1)} %add.92), channel_id=1, source_target_pairs={{0,16},{4,20},{8,24},{12,28},{16,0},{20,4},{24,8},{28,12},{1,17},{... | collective-permute-start | bytes 147464 | tf_op jit(solution)/shard_map/ppermute | solution.py:599
  336.4 0.7 copy-start.14
  338.9 12.1 %collective-permute-start.11 = (bf16[6,48,384]{2,1,0:T(8,128)(2,1)}, bf16[6,48,384]{2,1,0:T(8,128)(2,1)S(1)}, u32[]{:S(2)}, u32[]{:S(2)}) collective-permute-start(bf16[6,48,384]{2,1,0:T(8,128)(2,1)} %third_rest.1.refs_5_), channel_id=1, source_target_pairs={{0,1},{1,0},{2,3},{3,2},{4,5},{5,4},{6,7},{7,6},{8,9},{9,8},{10,11... | collective-permute-start | bytes 663560 | tf_op jit(solution)/shard_map/ppermute | solution.py:604
  346.3 4.7 %copy-start.12 = (bf16[8,48,384]{2,1,0:T(8,128)(2,1)}, bf16[8,48,384]{2,1,0:T(8,128)(2,1)S(1)}, u32[]{:S(2)}) copy-start(bf16[8,48,384]{2,1,0:T(8,128)(2,1)S(1)} %collective-permute-done.5.refs_2_) | copy-start | bytes 884740
  346.3 4.7 %copy-start.8 = (bf16[10,48,384]{2,1,0:T(8,128)(2,1)}, bf16[10,48,384]{2,1,0:T(8,128)(2,1)S(1)}, u32[]{:S(2)}) copy-start(bf16[10,48,384]{2,1,0:T(8,128)(2,1)S(1)} %collective-permute-done.8.refs_4_) | copy-start | bytes 1105924
  351.0 0.7 copy-start.16
  355.3 3.8 copy-start.7
  355.3 13.7 %copy-start.18 = (f32[9216]{0:T(1024)S(1)}, f32[9216]{0:T(1024)}, u32[]{:S(2)}) copy-start(f32[9216]{0:T(1024)} %param.17) | copy-start | bytes 110596
  355.3 13.7 %copy-start.20 = (f32[9216]{0:T(1024)S(1)}, f32[9216]{0:T(1024)}, u32[]{:S(2)}) copy-start(f32[9216]{0:T(1024)} %param.18) | copy-start | bytes 110596
  355.3 26.8 %all-to-all-start.2 = ((bf16[8,6,48,384]{3,2,1,0:T(8,128)(2,1)}), bf16[8,6,48,384]{3,2,1,0:T(8,128)(2,1)S(1)}, u32[]{:S(2)}, u32[]{:S(2)}) async-start(bf16[8,6,48,384]{3,2,1,0:T(8,128)(2,1)} %lay.1), calls=%async_computation.3 | async-start | bytes 3538944 | tf_op jit(solution)/shard_map/all_to_all | solution.py:937
  359.0 4.2 %collective-permute-start.15 = (f32[16,768]{1,0:T(8,128)S(1)}, f32[16,768]{1,0:T(8,128)S(1)}, u32[]{:S(2)}, u32[]{:S(2)}) collective-permute-start(f32[16,768]{1,0:T(8,128)S(1)} %copy-done.7), channel_id=1, source_target_pairs={{0,1},{1,0},{2,3},{3,2},{4,5},{5,4},{6,7},{7,6},{8,9},{9,8},{10,11... | collective-permute-start | bytes 147464 | tf_op jit(solution)/shard_map/ppermute | solution.py:604
  363.2 5.3 %collective-permute-start.16 = (f32[16,768]{1,0:T(8,128)S(1)}, f32[16,768]{1,0:T(8,128)S(1)}, u32[]{:S(2)}, u32[]{:S(2)}) collective-permute-start(f32[16,768]{1,0:T(8,128)S(1)} %add.94), channel_id=1, source_target_pairs={{0,2},{1,3},{2,0},{3,1},{4,6},{5,7},{6,4},{7,5},{8,10},{9,11},{10,... | collective-permute-start | bytes 147464 | tf_op jit(solution)/shard_map/ppermute | solution.py:604
  368.5 21.8 %copy-start.19 = (f32[9216]{0:T(1024)}, f32[9216]{0:T(1024)S(1)}, u32[]{:S(2)}) copy-start(f32[9216]{0:T(1024)S(1)} %reshape.56) | copy-start | bytes 110596
  382.1 1.2 copy-start.1
Sparse Core Ops, SparseCore 0:
  11.7 105.9 all-gather.2
  119.8 38.4 all-gather.4
  170.7 52.0 reduce-scatter.1
